TPU v7x, 128 devices: a whole 4x4x4 slice. The times are simulated.
128 devices in a mesh: bucket: 8 (over z, core), shard: 16 (over x, y).
Axes of the slice: x: 4, y: 4, z: 4, core: 2. Of those that a mesh axis runs over, the one named last changes fastest.
Arguments:
- head_rows: bfloat16 [65536, 400], P(('bucket', 'shard'))
- tail_rows: bfloat16 [65536, 400], P(('bucket', 'shard')), may hold values from -2.5 to 2.5
- rel_ids: int32 [65536], P(('bucket', 'shard')), may hold values from 0 to 511
- relations: float32 [512, 400], replicated, as said below
- edge_weights: float32 [65536], P(('bucket', 'shard')), may hold values from 0.5 to 2
- neg_rows: bfloat16 [8192, 400], P('bucket')
- send_slots: int32 [16384, 16], P(('bucket', 'shard')), may hold values from -1 to 1023, as said below
- dest_rows: int32 [16384, 16], P(('bucket', 'shard')), may hold values from 0 to 1024, as said below
Outputs:
- ent_grad: float32 [131072, 400], P(('bucket', 'shard'))
- neg_grad: float32 [8192, 400], P(('bucket', 'shard'))
- rel_grad: float32 [512, 400], replicated
Inputs may be any that keep to these rules, and one draw needn't show every extreme that they name: `send_slots`: each of a device's 2 * 512 edge ends stands in exactly one of its slots; -1 marks an empty slot. `dest_rows`: A row below 1024 in every used slot; exactly 1024 in every empty slot. `relations`: the magnitude of every relation's real part is at least 0.5.
All inputs are finite; a program needn't handle non-finite values.
Results may differ from a plain program's by a relative error of at most 0.0035.
Values may be sent and summed in bfloat16 or wider, within the bound.
A program may use at most 128 MiB of HBM per device.

v0:
```python
import functools

import jax
import jax.numpy as jnp
from jax import lax
from jax.experimental import pallas as pl
from jax.experimental.pallas import tpu as pltpu
from jax.sharding import PartitionSpec as P

D = 400
HALF = 200
DP = 512
E_DEV = 512
ENT_DEV = 1024
REL = 512
NEG_DEV = 1024
SLOT = 16
NB = 8
NS = 16
NZ = 4
EC = 256
NEG_OWN = 64

MESH = pl.DeviceIdType.MESH
F32 = jnp.float32
BF16 = jnp.bfloat16

(Q1_S, SQ1_S, Q2_S, SQ2_S, Q3_S, SQ3_S, ST1_S, O1_S, SC1_S, O2_S, ST2_S, O3_S, SC2_S,
 RC_S, R2_S, R3_S, R4_S, R5_S, ENT_S, Z1_S, X1_S, Y1_S, Z2_S, X2_S, Y2_S, GZ_S, GX_S, GY_S) = range(28)


def nt(a, b):
    return lax.dot_general(a, b, (((1,), (1,)), ((), ())), preferred_element_type=F32)


def nn(a, b):
    return jnp.dot(a, b, preferred_element_type=F32)


def iota(shape, dim):
    return lax.broadcasted_iota(jnp.int32, shape, dim)


def hot_where(mask):
    return mask.astype(F32).astype(BF16)


def wait_bytes(ref, sem):
    pltpu.make_async_copy(ref, ref, sem).wait()


def kernel(
    head, tail, ids, rel, wts, neg, slots, drows,
    ent_out, neg_out, rel_out,
    nbt, wide, nb, prob, qt, sq, hts, tts, rts, mb, st, st_in, sc, sc_in,
    ot, ot_pair, ot_own, o_sum, o_far, lt, qs, ends, rt_hi, rt_lo,
    packed, arrived, slot_col, dest_col,
    gz, gx, gy, rz1, rx1, ry1, az, ax, ay, rz2, rx2, ry2,
    rp, rp_in, r1b, r2in, r2all, rfin,
    send, recv,
):
    bucket, shard = lax.axis_index("bucket"), lax.axis_index("shard")
    z, c = bucket // 2, bucket % 2
    x, y = shard // 4, shard % 4
    oc = 1 - c
    me = bucket * NS + shard
    partner = (z * 2 + oc, shard)
    pair = ((z + 1 - 2 * (z % 2)) * 2 + c, shard)
    z_far = 3 - z
    far = (z_far * 2 + c, shard)

    def rcopy(src, dst, s_sem, r_sem, device):
        pltpu.make_async_remote_copy(
            src_ref=src, dst_ref=dst, send_sem=s_sem, recv_sem=r_sem,
            device_id=device, device_id_type=MESH,
        ).start()

    barrier = pltpu.get_barrier_semaphore()

    def greet(i, carry):
        d = lax.rem(me + i, NB * NS)
        pl.semaphore_signal(barrier, inc=1, device_id=(d // NS, d % NS), device_id_type=MESH)
        return carry

    lax.fori_loop(1, NB * NS, greet, 0)

    for g in range(8):
        qt[g, D:DP, :] = jnp.zeros((DP - D, EC), BF16)
    wide[D:, :] = jnp.ones((16, NEG_DEV), BF16)

    for i in range(8):
        nbt[i] = neg[:, i * 128 : (i + 1) * 128]

    rel_1 = rel[...].astype(BF16)
    rest = rel[...] - rel_1.astype(F32)
    rel_2 = rest.astype(BF16)
    rel_3 = (rest - rel_2.astype(F32)).astype(BF16)
    for j in range(2):
        cols = slice(j * EC, (j + 1) * EC)
        h_t = head[:, cols].astype(F32)
        t_t = tail[:, cols].astype(F32)
        hot = hot_where(iota((REL, EC), 0) == ids[0:1, cols])
        r_t = (nn(rel_1, hot) + nn(rel_2, hot)) + nn(rel_3, hot)
        hre, him = h_t[:HALF], h_t[HALF:]
        rre, rim = r_t[:HALF], r_t[HALF:]
        q = jnp.concatenate([hre * rre - him * rim, hre * rim + him * rre], axis=0).astype(BF16)
        qt[2 * c + j, 0:D, :] = q
        sq[2 * c + j, 0:1, :] = jnp.sum(q.astype(F32) * t_t, axis=0, keepdims=True)
        sq[2 * c + j, 1:2, :] = wts[0:1, cols]
        sq[2 * c + j, 2:8, :] = jnp.zeros((6, EC), F32)
        hts[j] = h_t
        tts[j] = t_t
        rts[j] = r_t

    pl.semaphore_wait(barrier, NB * NS - 1)

    for i in (x, 4 + y):
        rcopy(nbt.at[i], nbt.at[8 + i], send.at[GZ_S], recv.at[GZ_S], far)
    mine, theirs, real = pl.ds(2 * c, 2), pl.ds(4 + 2 * c, 2), pl.ds(0, D)
    rcopy(qt.at[mine, real], qt.at[mine, real], send.at[Q1_S], recv.at[Q1_S], partner)
    rcopy(sq.at[mine], sq.at[mine], send.at[SQ1_S], recv.at[SQ1_S], partner)
    rcopy(qt.at[mine, real], qt.at[theirs, real], send.at[Q2_S], recv.at[Q2_S], pair)
    rcopy(sq.at[mine], sq.at[theirs], send.at[SQ2_S], recv.at[SQ2_S], pair)

    ones = jnp.ones((SLOT, 128), BF16)
    tables = []
    for ref in (slots, drows):
        value = ref[...].astype(F32)
        high = jnp.floor(value * (1.0 / 32.0))
        tables.append((high.astype(BF16), (value - 32.0 * high).astype(BF16)))

    def columns(b, carry):
        owner_hot = hot_where(iota((256, 128), 1) == iota((256, 128), 0) // SLOT + b * NS)
        keep = iota((256, SLOT), 1) == iota((256, SLOT), 0) % SLOT
        for (high, low), out in zip(tables, (slot_col, dest_col)):
            h = jnp.where(keep, nt(owner_hot, high), 0.0).astype(BF16)
            l = jnp.where(keep, nt(owner_hot, low), 0.0).astype(BF16)
            out[b] = 32.0 * nn(h, ones) + nn(l, ones)
        return carry

    lax.fori_loop(0, NB, columns, 0)
    nb[:, 384:DP] = jnp.zeros((NEG_DEV, 128), BF16)

    def flip(b):
        for i in range(8):
            part = nbt[b * 8 + i]
            wide[0:D, i * 128 : (i + 1) * 128] = part
            nb[i * 128 : (i + 1) * 128, 0:D] = part.astype(F32).T.astype(BF16)

    def block(b, two):

        chunks = (2 * two, 2 * two + 1)
        scores = [nn(nb[...], qt[g]) for g in chunks]
        for g, s in zip(chunks, scores):
            m = jnp.max(s, axis=0, keepdims=True)
            pb = jnp.exp(s - m).astype(BF16)
            prob[b, :, pl.ds(pl.multiple_of(g * EC, EC), EC)] = pb
            o = nn(wide[...], pb)
            l = o[D : D + 1]
            o = o[0:D]
            mb[b, g, 0:1, :] = m
            if b == 0:
                st[g, 0:1, :] = m
                st[g, 1:2, :] = l
                st[g, 2:8, :] = jnp.zeros((6, EC), F32)
                ot[g] = o
            else:
                m_old = st[g, 0:1, :]
                m_new = jnp.maximum(m_old, m)
                f_old = jnp.exp(m_old - m_new)
                f_new = jnp.exp(m - m_new)
                st[g, 0:1, :] = m_new
                st[g, 1:2, :] = st[g, 1:2, :] * f_old + l * f_new
                ot[g] = ot[g] * f_old + o * f_new

    flip(0)
    block(0, c)
    wait_bytes(nbt.at[pl.ds(8, 2)], recv.at[GZ_S])
    for i in (1, 3, 2):
        xx, yy = lax.rem(x + i, 4), lax.rem(y + i, 4)
        rcopy(nbt.at[8 + x], nbt.at[8 + x], send.at[GX_S], recv.at[GX_S], (bucket, xx * 4 + y))
        rcopy(nbt.at[12 + y], nbt.at[12 + y], send.at[GY_S], recv.at[GY_S], (bucket, x * 4 + yy))
    wait_bytes(qt.at[mine, real], recv.at[Q1_S])
    wait_bytes(sq.at[mine], recv.at[SQ1_S])
    block(0, oc)
    wait_bytes(qt.at[mine, real], recv.at[Q2_S])
    wait_bytes(sq.at[mine], recv.at[SQ2_S])
    rcopy(qt.at[theirs, real], qt.at[theirs, real], send.at[Q3_S], recv.at[Q3_S], partner)
    rcopy(sq.at[theirs], sq.at[theirs], send.at[SQ3_S], recv.at[SQ3_S], partner)
    block(0, 2 + c)
    wait_bytes(qt.at[mine, real], recv.at[Q3_S])
    wait_bytes(sq.at[mine], recv.at[SQ3_S])
    block(0, 2 + oc)
    wait_bytes(nbt.at[pl.ds(8, 3)], recv.at[GX_S])
    wait_bytes(nbt.at[pl.ds(8, 3)], recv.at[GY_S])
    flip(1)
    block(1, 2 + oc)
    rcopy(
        ot.at[pl.ds(4 + 2 * oc, 2)], ot_pair, send.at[O1_S], recv.at[O1_S], partner
    )
    block(1, 2 + c)
    own_half, pair_half = pl.ds(0, 4), pl.ds(4, 4)
    rcopy(st.at[pair_half], st_in.at[pair_half], send.at[ST1_S], recv.at[ST1_S], partner)

    def merge(g):
        m_a, m_b = st[g, 0:1, :], st_in[g, 0:1, :]
        m = jnp.maximum(m_a, m_b)
        f_a, f_b = jnp.exp(m_a - m), jnp.exp(m_b - m)
        sc[g, 0:1, :] = m
        sc[g, 1:2, :] = st[g, 1:2, :] * f_a + st_in[g, 1:2, :] * f_b
        sc[g, 2:8, :] = jnp.zeros((6, EC), F32)
        return f_a, f_b

    block(1, oc)
    rcopy(ot.at[pl.ds(2 * oc, 2)], ot_own, send.at[O3_S], recv.at[O3_S], partner)
    wait_bytes(st_in.at[pair_half], recv.at[ST1_S])
    wait_bytes(ot_pair, recv.at[O1_S])
    for g in range(4, 8):
        merge(g)
    for j in range(2):
        f_a, f_b = merge(4 + 2 * c + j)
        o_sum[j] = (ot[4 + 2 * c + j] * f_a + ot_pair[j] * f_b).astype(BF16)
    rcopy(sc.at[pair_half], sc_in.at[own_half], send.at[SC1_S], recv.at[SC1_S], pair)
    block(1, c)
    rcopy(st.at[own_half], st_in.at[own_half], send.at[ST2_S], recv.at[ST2_S], partner)
    wait_bytes(st_in.at[own_half], recv.at[ST2_S])
    for g in range(4):
        merge(g)
    rcopy(sc.at[own_half], sc_in.at[pair_half], send.at[SC2_S], recv.at[SC2_S], pair)
    rcopy(o_sum, o_far, send.at[O2_S], recv.at[O2_S], pair)
    wait_bytes(sc_in.at[own_half], recv.at[SC1_S])
    wait_bytes(sc_in.at[pair_half], recv.at[SC2_S])
    for g in range(8):
        pos = sq[g, 0:1, :]
        m0, m1 = sc[g, 0:1, :], sc_in[g, 0:1, :]
        top = jnp.maximum(pos, jnp.maximum(m0, m1))
        total = (
            jnp.exp(pos - top)
            + sc[g, 1:2, :] * jnp.exp(m0 - top)
            + sc_in[g, 1:2, :] * jnp.exp(m1 - top)
        )
        lt[g, 0:1, :] = top + jnp.log(total)

    def neg_block(b):
        for g in range(8):
            scale = sq[g, 1:2, :] * jnp.exp(mb[b, g, 0:1, :] - lt[g, 0:1, :])
            qs[:, g * EC : (g + 1) * EC] = (qt[g].astype(F32) * scale).astype(BF16)

        def rows_of(h, carry):
            rr = pl.ds(pl.multiple_of(h * 512, 512), 512)
            acc = nt(prob[b, rr, :], qs[...])
            for u in range(2):
                part = acc[u * 256 : (u + 1) * 256]
                gx[b, 2 * h + u] = part[:, 0:128].astype(BF16)
                for yy in range(4):
                    gy[b, yy, 2 * h + u] = part[yy * 64 : (yy + 1) * 64, 128:256].astype(BF16)
            gz[b, :, rr] = acc[:, 256:512].T[0 : D - 256].astype(BF16)
            return carry

        lax.fori_loop(0, 2, rows_of, 0)
        for i in (1, 3, 2):
            xx, yy = lax.rem(x + i, 4), lax.rem(y + i, 4)
            rcopy(gx.at[b, xx], rx1.at[x, b], send.at[X1_S], recv.at[X1_S], (bucket, xx * 4 + y))
            rcopy(gy.at[b, yy], ry1.at[y, b], send.at[Y1_S], recv.at[Y1_S], (bucket, x * 4 + yy))

    neg_block(1)
    rcopy(gz.at[1], rz1, send.at[Z1_S], recv.at[Z1_S], far)
    wait_bytes(ot_own, recv.at[O3_S])
    wait_bytes(o_far, recv.at[O2_S])
    ends[D:DP, :] = jnp.zeros((DP - D, 2 * E_DEV), BF16)
    for j in range(2):
        cols = slice(j * EC, (j + 1) * EC)
        tail_cols = slice(E_DEV + j * EC, E_DEV + (j + 1) * EC)
        g = 2 * c + j
        pos, w, ltot = sq[g, 0:1, :], sq[g, 1:2, :], lt[g, 0:1, :]
        pos_coef = w * (jnp.exp(pos - ltot) - 1.0)
        own = w * jnp.exp(st[g, 0:1, :] - ltot)
        other = w * jnp.exp(st_in[g, 0:1, :] - ltot)
        away = w * jnp.exp(sc_in[g, 0:1, :] - ltot)
        grad = pos_coef * tts[j] + ot[g] * own + ot_own[j] * other + o_far[j].astype(F32) * away
        gre, gim = grad[:HALF], grad[HALF:]
        rre, rim = rts[j, :HALF, :], rts[j, HALF:, :]
        hre, him = hts[j, :HALF, :], hts[j, HALF:, :]
        ends[0:D, cols] = jnp.concatenate(
            [gre * rre + gim * rim, gim * rre - gre * rim], axis=0
        ).astype(BF16)
        ends[0:D, tail_cols] = (pos_coef * qt[g, 0:D, :].astype(F32)).astype(BF16)
        term = jnp.concatenate([gre * hre + gim * him, gim * hre - gre * him], axis=0)
        hi = term.astype(BF16)
        rt_hi[:, cols] = hi
        rt_lo[:, cols] = (term - hi.astype(F32)).astype(BF16)

    my_slots = pl.ds(pl.multiple_of(me * SLOT, SLOT), SLOT)

    def pack(k, first):
        sel = []
        for u in range(2):
            sc_b = slot_col[lax.rem(bucket + 2 * k + u, NB)]
            sel.append(jnp.concatenate(
                [hot_where(sc_b == (iota((256, 128), 1) + 128 * t).astype(F32)) for t in range(8)],
                axis=1,
            ))
        rows = nt(jnp.concatenate(sel, axis=0), ends[...])
        for u in range(2):
            bb = lax.rem(bucket + 2 * k + u, NB)
            part = rows[u * 256 : (u + 1) * 256]
            dc = dest_col[bb]
            high = jnp.floor(dc * (1.0 / 32.0))
            lane = iota((256, 128), 1)
            code = jnp.where(lane == 16, high, jnp.where(lane == 17, dc - 32.0 * high, 0.0))
            packed[bb, :, 0:384] = part[:, 0:384].astype(BF16)
            packed[bb, :, 384:512] = (part[:, 384:512] + code).astype(BF16)
            for j in range(NS):
                ss = lax.rem(shard + j, NS)
                src = packed.at[bb, pl.ds(pl.multiple_of(ss * SLOT, SLOT), SLOT)]
                if first and u == 0 and j == 0:
                    pltpu.make_async_copy(src, arrived.at[my_slots], recv.at[ENT_S]).start()
                else:
                    rcopy(src, arrived.at[my_slots], send.at[ENT_S], recv.at[ENT_S], (bb, ss))

    def rel_chunk(r, carry):
        hot = hot_where(iota((128, E_DEV), 0) + r * 128 == ids[...])
        rp[pl.ds(pl.multiple_of(r * 128, 128), 128), :] = nt(hot, rt_hi[...]) + nt(hot, rt_lo[...])
        return carry

    lax.fori_loop(0, 4, rel_chunk, 0)
    rcopy(
        rp.at[pl.ds(pl.multiple_of(oc * 256, 256), 256)], rp_in, send.at[RC_S], recv.at[RC_S], partner
    )

    def pack_other(k, carry):
        pack(k, False)
        return carry

    pack(0, True)
    lax.fori_loop(1, 2, pack_other, 0)

    wait_bytes(rp_in, recv.at[RC_S])
    r1b[...] = (rp[pl.ds(pl.multiple_of(c * 256, 256), 256), :] + rp_in[...]).astype(BF16)
    for j in range(1, NS):
        ss = lax.rem(shard + j, NS)
        rows = r1b.at[pl.ds(pl.multiple_of(ss * 16, 16), 16)]
        rcopy(rows, r2in.at[shard], send.at[R2_S], recv.at[R2_S], (bucket, ss))
    r2in[shard] = r1b[pl.ds(pl.multiple_of(shard * 16, 16), 16), :]
    lax.fori_loop(2, NB // 2, pack_other, 0)

    neg_block(0)


    wait_bytes(r2in.at[pl.ds(0, NS - 1)], recv.at[R2_S])
    r2 = r2in[0].astype(F32)
    for i in range(1, NS):
        r2 = r2 + r2in[i].astype(F32)
    r2all[z] = r2
    for k in (1, 3, 2):
        zz = lax.rem(z + k, NZ)
        rcopy(r2all.at[z], r2all.at[z], send.at[R3_S], recv.at[R3_S], (zz * 2 + c, shard))

    my_rows = pl.ds(pl.multiple_of(shard * NEG_OWN, NEG_OWN), NEG_OWN)
    wait_bytes(rx1.at[pl.ds(0, 3)], recv.at[X1_S])
    for b in range(2):
        total = gx[b, x].astype(F32)
        for i in range(1, 4):
            total = total + rx1[lax.rem(x + i, 4), b].astype(F32)
        ax[b] = total.astype(BF16)
    for i in range(4):
        yy = lax.rem(y + i, 4)
        rows = pl.ds(pl.multiple_of(yy * NEG_OWN, NEG_OWN), NEG_OWN)
        if i:
            rcopy(ax.at[0, rows], rx2.at[y], send.at[X2_S], recv.at[X2_S], (bucket, x * 4 + yy))
        else:
            rx2[y] = ax[0, rows, :]
        rcopy(
            ax.at[1, rows], rx2.at[4 + y], send.at[X2_S], recv.at[X2_S], (z_far * 2 + c, x * 4 + yy)
        )
    wait_bytes(r2all.at[pl.ds(0, 3)], recv.at[R3_S])
    rel_row = pl.ds(pl.multiple_of(c * 256 + shard * 16, 16), 16)
    rfin[rel_row, :] = (((r2all[0] + r2all[1]) + r2all[2]) + r2all[3]).astype(BF16)
    for j in range(1, NS):
        ss = lax.rem(shard + j, NS)
        rcopy(rfin.at[rel_row], rfin.at[rel_row], send.at[R4_S], recv.at[R4_S], (bucket, ss))

    wait_bytes(ry1.at[pl.ds(0, 3)], recv.at[Y1_S])
    for b in range(2):
        total = gy[b, y].astype(F32)
        for i in range(1, 4):
            total = total + ry1[lax.rem(y + i, 4), b].astype(F32)
        ay[b] = total.astype(BF16)
    for i in range(4):
        xx = lax.rem(x + i, 4)
        if i:
            rcopy(ay.at[0, xx], ry2.at[x], send.at[Y2_S], recv.at[Y2_S], (bucket, xx * 4 + y))
        else:
            ry2[x] = ay[0, x]
        rcopy(
            ay.at[1, xx], ry2.at[4 + x], send.at[Y2_S], recv.at[Y2_S], (z_far * 2 + c, xx * 4 + y)
        )
    wait_bytes(rz1, recv.at[Z1_S])

    def sum_z(r, carry):
        rr = pl.ds(pl.multiple_of(r * 256, 256), 256)
        total = gz[0, :, rr].astype(F32) + rz1[:, rr].astype(F32)
        wide_sum = jnp.concatenate([total, jnp.zeros((256 - (D - 256), 256), F32)], axis=0)
        az[rr, :] = wide_sum.T.astype(BF16)
        return carry

    lax.fori_loop(0, 4, sum_z, 0)
    for j in range(1, NS):
        ss = lax.rem(shard + j, NS)
        rows = az.at[pl.ds(pl.multiple_of(ss * NEG_OWN, NEG_OWN), NEG_OWN)]
        rcopy(rows, rz2.at[shard], send.at[Z2_S], recv.at[Z2_S], (bucket, ss))
    rz2[shard] = az[my_rows, :]

    wait_bytes(arrived, recv.at[ENT_S])
    lane = iota((8, DP), 1)
    unit = jnp.where(lane == D, 32.0, jnp.where(lane == D + 1, 1.0, 0.0)).astype(BF16)
    row_ids = nt(unit, arrived[...])[0:1, :]

    def scatter(r, carry):
        hot = hot_where((iota((512, 2048), 0) + r * 512).astype(F32) == row_ids)
        got = nn(hot, arrived[...])
        ent_out[:, pl.ds(pl.multiple_of(r * 512, 512), 512)] = got.T[0:D]
        return carry

    lax.fori_loop(0, 2, scatter, 0)

    wait_bytes(rfin.at[pl.ds(0, 240)], recv.at[R4_S])
    half_rel = rfin.at[pl.ds(pl.multiple_of(c * 256, 256), 256)]
    rcopy(half_rel, half_rel, send.at[R5_S], recv.at[R5_S], partner)

    def sum16(ref):
        total = ref[0].astype(F32)
        for i in range(1, ref.shape[0]):
            total = total + ref[i].astype(F32)
        return total

    wait_bytes(rx2.at[pl.ds(0, 7)], recv.at[X2_S])
    neg_out[:, 0:128] = sum16(rx2)
    wait_bytes(ry2.at[pl.ds(0, 7)], recv.at[Y2_S])
    neg_out[:, 128:256] = sum16(ry2)
    wait_bytes(rz2.at[pl.ds(0, NS - 1)], recv.at[Z2_S])
    neg_out[:, 256:D] = sum16(rz2)[:, 0 : D - 256]

    wait_bytes(half_rel, recv.at[R5_S])
    for r in range(4):
        rr = slice(r * 128, (r + 1) * 128)
        wide_rel = jnp.concatenate([rfin[rr, :].astype(F32), jnp.zeros((128, DP - D), F32)], axis=1)
        rel_out[:, rr] = wide_rel.T[0:D]

    wait_bytes(nbt.at[pl.ds(0, 2)], send.at[GZ_S])
    wait_bytes(nbt.at[pl.ds(0, 3)], send.at[GX_S])
    wait_bytes(nbt.at[pl.ds(0, 3)], send.at[GY_S])
    for number in (Q1_S, Q2_S, Q3_S):
        wait_bytes(qt.at[mine, real], send.at[number])
    for number in (SQ1_S, SQ2_S, SQ3_S):
        wait_bytes(sq.at[mine], send.at[number])
    for number in (ST1_S, ST2_S, SC1_S, SC2_S):
        wait_bytes(st.at[own_half], send.at[number])
    wait_bytes(ot_pair, send.at[O1_S])
    wait_bytes(o_far, send.at[O2_S])
    wait_bytes(ot_own, send.at[O3_S])
    wait_bytes(arrived.at[pl.ds(0, 2048 - SLOT)], send.at[ENT_S])
    wait_bytes(rp_in, send.at[RC_S])
    wait_bytes(r2in.at[pl.ds(0, NS - 1)], send.at[R2_S])
    wait_bytes(r2all.at[pl.ds(0, 3)], send.at[R3_S])
    wait_bytes(rfin.at[pl.ds(0, 240)], send.at[R4_S])
    wait_bytes(half_rel, send.at[R5_S])
    wait_bytes(rz1, send.at[Z1_S])
    wait_bytes(rx1.at[pl.ds(0, 3)], send.at[X1_S])
    wait_bytes(ry1.at[pl.ds(0, 3)], send.at[Y1_S])
    wait_bytes(rx2.at[pl.ds(0, 7)], send.at[X2_S])
    wait_bytes(ry2.at[pl.ds(0, 7)], send.at[Y2_S])
    wait_bytes(rz2.at[pl.ds(0, NS - 1)], send.at[Z2_S])


SCRATCH = [
    ((16, D, 128), BF16),
    ((D + 16, NEG_DEV), BF16),
    ((NEG_DEV, DP), BF16),
    ((2, NEG_DEV, 8 * EC), BF16),
    ((8, DP, EC), BF16),
    ((8, 8, EC), F32),
    ((2, D, EC), F32),
    ((2, D, EC), F32),
    ((2, D, EC), F32),
    ((2, 8, 8, EC), F32),
    ((8, 8, EC), F32),
    ((8, 8, EC), F32),
    ((8, 8, EC), F32),
    ((8, 8, EC), F32),
    ((8, D, EC), F32),
    ((2, D, EC), F32),
    ((2, D, EC), F32),
    ((2, D, EC), BF16),
    ((2, D, EC), BF16),
    ((8, 8, EC), F32),
    ((DP, 8 * EC), BF16),
    ((DP, 2 * E_DEV), BF16),
    ((D, E_DEV), BF16),
    ((D, E_DEV), BF16),
    ((NB, 256, DP), BF16),
    ((2048, DP), BF16),
    ((NB, 256, 128), F32),
    ((NB, 256, 128), F32),
    ((2, D - 256, NEG_DEV), BF16),
    ((2, 4, 256, 128), BF16),
    ((2, 4, 4, NEG_OWN, 128), BF16),
    ((D - 256, NEG_DEV), BF16),
    ((4, 2, 256, 128), BF16),
    ((4, 2, 4, NEG_OWN, 128), BF16),
    ((NEG_DEV, 256), BF16),
    ((2, 256, 128), BF16),
    ((2, 4, NEG_OWN, 128), BF16),
    ((NS, NEG_OWN, 256), BF16),
    ((8, NEG_OWN, 128), BF16),
    ((8, NEG_OWN, 128), BF16),
    ((REL, D), F32),
    ((REL // 2, D), F32),
    ((REL // 2, D), BF16),
    ((NS, 16, D), BF16),
    ((NZ, 16, D), F32),
    ((REL, D), BF16),
]


def per_device(
    head_rows, tail_rows, rel_ids, relations, edge_weights, neg_rows, send_slots, dest_rows
):
    vmem = pl.BlockSpec(memory_space=pltpu.VMEM)
    ent_t, neg_grad, rel_t = pl.pallas_call(
        kernel,
        out_shape=(
            jax.ShapeDtypeStruct((D, ENT_DEV), F32),
            jax.ShapeDtypeStruct((NEG_OWN, D), F32),
            jax.ShapeDtypeStruct((D, REL), F32),
        ),
        in_specs=[vmem] * 8,
        out_specs=(vmem,) * 3,
        scratch_shapes=[pltpu.VMEM(shape, dtype) for shape, dtype in SCRATCH]
        + [
            pltpu.SemaphoreType.DMA((28,)),
            pltpu.SemaphoreType.DMA((28,)),
        ],
        compiler_params=pltpu.CompilerParams(
            collective_id=0, has_side_effects=True, vmem_limit_bytes=60 * 1024 * 1024
        ),
        cost_estimate=pl.CostEstimate(
            flops=2 * 3 * 1024 * 4096 * 400, bytes_accessed=8 * 1024 * 1024, transcendentals=1024 * 4096
        ),
        name="complex_backward",
    )(
        head_rows.T,
        tail_rows.T,
        rel_ids.reshape(1, E_DEV),
        relations.T,
        edge_weights.reshape(1, E_DEV),
        neg_rows.T,
        send_slots.T,
        dest_rows.T,
    )
    return ent_t.T, neg_grad, rel_t.T


def solution(mesh):
    return jax.shard_map(
        per_device,
        mesh=mesh,
        in_specs=(
            P(("bucket", "shard"), None),
            P(("bucket", "shard"), None),
            P(("bucket", "shard")),
            P(),
            P(("bucket", "shard")),
            P("bucket", None),
            P(("bucket", "shard"), None),
            P(("bucket", "shard"), None),
        ),
        out_specs=(P(("bucket", "shard"), None), P(("bucket", "shard"), None), P()),
        check_vma=False,
    )
```

profile of v0, /device:TPU:0, one launch (start us, length us, event | category | flops | bytes accessed | tf_op | source)
XLA Modules:
  0.0 102.0 jit_solution(3053545760126733592)
XLA Ops:
  0.6 97.0 %complex_backward.1 = (f32[400,1024]{1,0:T(8,128)}, f32[64,400]{1,0:T(8,128)}, f32[400,512]{1,0:T(8,128)}) custom-call(bf16[400,512]{1,0:T(8,128)(2,1)} %bitcast.14, bf16[400,512]{1,0:T(8,128)(2,1)} %bitcast.15, s32[1,512]{1,0:T(1,128)} %bitcast.18, f32[400,512]{1,0:T(8,128)} %bitcast.12, f32[1,512]{1,0:T(1,128)} %bitcast.19, bf16[400,1024]{1,0:T(8,128)(2,1)} %bitcast.13, ...), custom_call_target="tpu_custom_call" | custom-call | flops 10066329600 | bytes 8388608 | tf_op jit(solution)/shard_map/complex_backward/pallas_call | solution.py:530
  97.6 0.0 copy-start.1
  97.6 0.0 copy-start
  97.6 2.9 %copy.14 = f32[1024,400]{0,1:T(8,128)} copy(f32[1024,400]{0,1:T(8,128)} %bitcast.10) | data formatting | bytes 3276800
  100.5 0.0 copy-done.1
  100.5 0.7 copy.15
  101.2 0.0 copy-done
  101.2 0.9 copy.16
Async XLA Ops:
  97.6 2.9 %copy-start.1 = (f32[64,400]{1,0:T(8,128)S(1)}, f32[64,400]{1,0:T(8,128)}, u32[]{:S(2)}) copy-start(f32[64,400]{1,0:T(8,128)} %get-tuple-element.13) | copy-start | bytes 307204
  97.6 3.5 %copy-start = (f32[400,512]{1,0:T(8,128)S(1)}, f32[400,512]{1,0:T(8,128)}, u32[]{:S(2)}) copy-start(f32[400,512]{1,0:T(8,128)} %get-tuple-element.8) | copy-start | bytes 2457604
where the time goes:
time: 104 us; the launch traced here: 102 us
  Pallas kernels  97 us (93%)
  local copies, waits for them, and re-layouts  4.42 us (4%)
    pallas_call x1, Pallas kernels, per_device(): pl.pallas_call(kernel, out_shape=(jax.ShapeDtypeStruct((D, ENT_DEV), F32)...  97 us
    unnamed x7, local copies, waits for them, and re-layouts  4.42 us

commit v1 on v0

--- a/solution.py
+++ b/solution.py
@@ -26,7 +26,7 @@
 BF16 = jnp.bfloat16
 
 (Q1_S, SQ1_S, Q2_S, SQ2_S, Q3_S, SQ3_S, ST1_S, O1_S, SC1_S, O2_S, ST2_S, O3_S, SC2_S,
- RC_S, R2_S, R3_S, R4_S, R5_S, ENT_S, Z1_S, X1_S, Y1_S, Z2_S, X2_S, Y2_S, GZ_S, GX_S, GY_S) = range(28)
+ RC_S, R2_S, R3_S, R4_S, R5_S, ENT_S, Z1_S, X1_S, Y1_S, Z2_S, X2_S, Y2_S, GZ_S, GX_S, GY_S, O4_S) = range(29)
 
 
 def nt(a, b):
@@ -51,13 +51,13 @@
 
 def kernel(
     head, tail, ids, rel, wts, neg, slots, drows,
-    ent_out, neg_out, rel_out,
+    arrived_out, rx2_out, ry2_out, rz2_out, rel_sum_out,
     nbt, wide, nb, prob, qt, sq, hts, tts, rts, mb, st, st_in, sc, sc_in,
     ot, ot_pair, ot_own, o_sum, o_far, lt, qs, ends, rt_hi, rt_lo,
     packed, arrived, slot_col, dest_col,
     gz, gx, gy, rz1, rx1, ry1, az, ax, ay, rz2, rx2, ry2,
     rp, rp_in, r1b, r2in, r2all, rfin,
-    send, recv,
+    send, recv, known, out_sem,
 ):
     bucket, shard = lax.axis_index("bucket"), lax.axis_index("shard")
     z, c = bucket // 2, bucket % 2
@@ -77,12 +77,15 @@
 
     barrier = pltpu.get_barrier_semaphore()
 
-    def greet(i, carry):
-        d = lax.rem(me + i, NB * NS)
-        pl.semaphore_signal(barrier, inc=1, device_id=(d // NS, d % NS), device_id_type=MESH)
-        return carry
-
-    lax.fori_loop(1, NB * NS, greet, 0)
+    x_peers = [(bucket, lax.rem(x + i, 4) * 4 + y) for i in (1, 2, 3)]
+    y_peers = [(bucket, x * 4 + lax.rem(y + i, 4)) for i in (1, 2, 3)]
+    friends = [partner, pair, far] + x_peers + y_peers
+
+    def tell(sem, devices):
+        for device in devices:
+            pl.semaphore_signal(sem, inc=1, device_id=device, device_id_type=MESH)
+
+    tell(barrier, friends)
 
     for g in range(8):
         qt[g, D:DP, :] = jnp.zeros((DP - D, EC), BF16)
@@ -112,7 +115,8 @@
         tts[j] = t_t
         rts[j] = r_t
 
-    pl.semaphore_wait(barrier, NB * NS - 1)
+    pl.semaphore_wait(barrier, len(friends))
+    tell(known.at[0], y_peers)
 
     for i in (x, 4 + y):
         rcopy(nbt.at[i], nbt.at[8 + i], send.at[GZ_S], recv.at[GZ_S], far)
@@ -175,6 +179,8 @@
 
     flip(0)
     block(0, c)
+    pl.semaphore_wait(known.at[0], 3)
+    tell(known.at[1], (pair, far))
     wait_bytes(nbt.at[pl.ds(8, 2)], recv.at[GZ_S])
     for i in (1, 3, 2):
         xx, yy = lax.rem(x + i, 4), lax.rem(y + i, 4)
@@ -183,6 +189,8 @@
     wait_bytes(qt.at[mine, real], recv.at[Q1_S])
     wait_bytes(sq.at[mine], recv.at[SQ1_S])
     block(0, oc)
+    pl.semaphore_wait(known.at[1], 2)
+    tell(known.at[2], (pair, far))
     wait_bytes(qt.at[mine, real], recv.at[Q2_S])
     wait_bytes(sq.at[mine], recv.at[SQ2_S])
     rcopy(qt.at[theirs, real], qt.at[theirs, real], send.at[Q3_S], recv.at[Q3_S], partner)
@@ -195,6 +203,8 @@
     wait_bytes(nbt.at[pl.ds(8, 3)], recv.at[GY_S])
     flip(1)
     block(1, 2 + oc)
+    pl.semaphore_wait(known.at[2], 2)
+    tell(known.at[3], (partner,))
     rcopy(
         ot.at[pl.ds(4 + 2 * oc, 2)], ot_pair, send.at[O1_S], recv.at[O1_S], partner
     )
@@ -212,6 +222,7 @@
         return f_a, f_b
 
     block(1, oc)
+    pl.semaphore_wait(known.at[3], 1)
     rcopy(ot.at[pl.ds(2 * oc, 2)], ot_own, send.at[O3_S], recv.at[O3_S], partner)
     wait_bytes(st_in.at[pair_half], recv.at[ST1_S])
     wait_bytes(ot_pair, recv.at[O1_S])
@@ -220,6 +231,7 @@
     for j in range(2):
         f_a, f_b = merge(4 + 2 * c + j)
         o_sum[j] = (ot[4 + 2 * c + j] * f_a + ot_pair[j] * f_b).astype(BF16)
+    rcopy(o_sum.at[0], o_far.at[0], send.at[O4_S], recv.at[O4_S], pair)
     rcopy(sc.at[pair_half], sc_in.at[own_half], send.at[SC1_S], recv.at[SC1_S], pair)
     block(1, c)
     rcopy(st.at[own_half], st_in.at[own_half], send.at[ST2_S], recv.at[ST2_S], partner)
@@ -227,7 +239,7 @@
     for g in range(4):
         merge(g)
     rcopy(sc.at[own_half], sc_in.at[pair_half], send.at[SC2_S], recv.at[SC2_S], pair)
-    rcopy(o_sum, o_far, send.at[O2_S], recv.at[O2_S], pair)
+    rcopy(o_sum.at[1], o_far.at[1], send.at[O2_S], recv.at[O2_S], pair)
     wait_bytes(sc_in.at[own_half], recv.at[SC1_S])
     wait_bytes(sc_in.at[pair_half], recv.at[SC2_S])
     for g in range(8):
@@ -266,7 +278,8 @@
     neg_block(1)
     rcopy(gz.at[1], rz1, send.at[Z1_S], recv.at[Z1_S], far)
     wait_bytes(ot_own, recv.at[O3_S])
-    wait_bytes(o_far, recv.at[O2_S])
+    wait_bytes(o_far.at[0], recv.at[O4_S])
+    wait_bytes(o_far.at[1], recv.at[O2_S])
     ends[D:DP, :] = jnp.zeros((DP - D, 2 * E_DEV), BF16)
     for j in range(2):
         cols = slice(j * EC, (j + 1) * EC)
@@ -342,9 +355,8 @@
         rows = r1b.at[pl.ds(pl.multiple_of(ss * 16, 16), 16)]
         rcopy(rows, r2in.at[shard], send.at[R2_S], recv.at[R2_S], (bucket, ss))
     r2in[shard] = r1b[pl.ds(pl.multiple_of(shard * 16, 16), 16), :]
+    neg_block(0)
     lax.fori_loop(2, NB // 2, pack_other, 0)
-
-    neg_block(0)
 
 
     wait_bytes(r2in.at[pl.ds(0, NS - 1)], recv.at[R2_S])
@@ -411,41 +423,22 @@
         rcopy(rows, rz2.at[shard], send.at[Z2_S], recv.at[Z2_S], (bucket, ss))
     rz2[shard] = az[my_rows, :]
 
+    def give(src, dst, sem):
+        pltpu.make_async_copy(src, dst, sem).start()
+
     wait_bytes(arrived, recv.at[ENT_S])
-    lane = iota((8, DP), 1)
-    unit = jnp.where(lane == D, 32.0, jnp.where(lane == D + 1, 1.0, 0.0)).astype(BF16)
-    row_ids = nt(unit, arrived[...])[0:1, :]
-
-    def scatter(r, carry):
-        hot = hot_where((iota((512, 2048), 0) + r * 512).astype(F32) == row_ids)
-        got = nn(hot, arrived[...])
-        ent_out[:, pl.ds(pl.multiple_of(r * 512, 512), 512)] = got.T[0:D]
-        return carry
-
-    lax.fori_loop(0, 2, scatter, 0)
-
+    give(arrived, arrived_out, out_sem.at[0])
     wait_bytes(rfin.at[pl.ds(0, 240)], recv.at[R4_S])
     half_rel = rfin.at[pl.ds(pl.multiple_of(c * 256, 256), 256)]
     rcopy(half_rel, half_rel, send.at[R5_S], recv.at[R5_S], partner)
-
-    def sum16(ref):
-        total = ref[0].astype(F32)
-        for i in range(1, ref.shape[0]):
-            total = total + ref[i].astype(F32)
-        return total
-
     wait_bytes(rx2.at[pl.ds(0, 7)], recv.at[X2_S])
-    neg_out[:, 0:128] = sum16(rx2)
+    give(rx2, rx2_out, out_sem.at[1])
     wait_bytes(ry2.at[pl.ds(0, 7)], recv.at[Y2_S])
-    neg_out[:, 128:256] = sum16(ry2)
+    give(ry2, ry2_out, out_sem.at[2])
     wait_bytes(rz2.at[pl.ds(0, NS - 1)], recv.at[Z2_S])
-    neg_out[:, 256:D] = sum16(rz2)[:, 0 : D - 256]
-
+    give(rz2, rz2_out, out_sem.at[3])
     wait_bytes(half_rel, recv.at[R5_S])
-    for r in range(4):
-        rr = slice(r * 128, (r + 1) * 128)
-        wide_rel = jnp.concatenate([rfin[rr, :].astype(F32), jnp.zeros((128, DP - D), F32)], axis=1)
-        rel_out[:, rr] = wide_rel.T[0:D]
+    give(rfin, rel_sum_out, out_sem.at[4])
 
     wait_bytes(nbt.at[pl.ds(0, 2)], send.at[GZ_S])
     wait_bytes(nbt.at[pl.ds(0, 3)], send.at[GX_S])
@@ -457,7 +450,8 @@
     for number in (ST1_S, ST2_S, SC1_S, SC2_S):
         wait_bytes(st.at[own_half], send.at[number])
     wait_bytes(ot_pair, send.at[O1_S])
-    wait_bytes(o_far, send.at[O2_S])
+    wait_bytes(o_far.at[0], send.at[O4_S])
+    wait_bytes(o_far.at[1], send.at[O2_S])
     wait_bytes(ot_own, send.at[O3_S])
     wait_bytes(arrived.at[pl.ds(0, 2048 - SLOT)], send.at[ENT_S])
     wait_bytes(rp_in, send.at[RC_S])
@@ -471,6 +465,59 @@
     wait_bytes(rx2.at[pl.ds(0, 7)], send.at[X2_S])
     wait_bytes(ry2.at[pl.ds(0, 7)], send.at[Y2_S])
     wait_bytes(rz2.at[pl.ds(0, NS - 1)], send.at[Z2_S])
+    wait_bytes(arrived, out_sem.at[0])
+    wait_bytes(rx2, out_sem.at[1])
+    wait_bytes(ry2, out_sem.at[2])
+    wait_bytes(rz2, out_sem.at[3])
+    wait_bytes(rfin, out_sem.at[4])
+
+
+def finish(
+    arrived_in, rx2_in, ry2_in, rz2_in, rel_in, ent_out, neg_out, rel_out,
+    arrived, rx2, ry2, rz2, rel_sum, ent, neg_sum, rel_t, in_sem, out_sem,
+):
+    loads = [
+        pltpu.make_async_copy(src, dst, in_sem.at[i])
+        for i, (src, dst) in enumerate((
+            (rel_in, rel_sum), (arrived_in, arrived), (rx2_in, rx2), (ry2_in, ry2), (rz2_in, rz2)
+        ))
+    ]
+    for load in loads:
+        load.start()
+    loads[0].wait()
+    for r in range(4):
+        rows = rel_sum[r * 128 : (r + 1) * 128, :].astype(F32)
+        wide = jnp.concatenate([rows, jnp.zeros((128, DP - D), F32)], axis=1)
+        rel_t[:, r * 128 : (r + 1) * 128] = wide.T[0:D]
+    stores = [pltpu.make_async_copy(rel_t, rel_out, out_sem.at[0])]
+    stores[0].start()
+
+    loads[1].wait()
+    lane = iota((8, 128), 1)
+    unit = jnp.where(lane == D - 384, 32.0, jnp.where(lane == D - 383, 1.0, 0.0)).astype(BF16)
+    row_ids = nt(unit, arrived[:, 384:DP])[0:1, :]
+    for r in range(2):
+        hot = hot_where((iota((512, 2048), 0) + r * 512).astype(F32) == row_ids)
+        ent[r] = nn(hot, arrived[...]).T[0:D]
+        store = pltpu.make_async_copy(ent.at[r], ent_out.at[:, pl.ds(r * 512, 512)], out_sem.at[1 + r])
+        store.start()
+        stores.append(store)
+
+    def sum_all(ref):
+        total = ref[0].astype(F32)
+        for i in range(1, ref.shape[0]):
+            total = total + ref[i].astype(F32)
+        return total
+
+    for load in loads[2:]:
+        load.wait()
+    neg_sum[:, 0:128] = sum_all(rx2)
+    neg_sum[:, 128:256] = sum_all(ry2)
+    neg_sum[:, 256:D] = sum_all(rz2)[:, 0 : D - 256]
+    stores.append(pltpu.make_async_copy(neg_sum, neg_out, out_sem.at[3]))
+    stores[-1].start()
+    for store in stores:
+        store.wait()
 
 
 SCRATCH = [
@@ -527,19 +574,24 @@
     head_rows, tail_rows, rel_ids, relations, edge_weights, neg_rows, send_slots, dest_rows
 ):
     vmem = pl.BlockSpec(memory_space=pltpu.VMEM)
-    ent_t, neg_grad, rel_t = pl.pallas_call(
+    anywhere = pl.BlockSpec(memory_space=pl.ANY)
+    results = pl.pallas_call(
         kernel,
         out_shape=(
-            jax.ShapeDtypeStruct((D, ENT_DEV), F32),
-            jax.ShapeDtypeStruct((NEG_OWN, D), F32),
-            jax.ShapeDtypeStruct((D, REL), F32),
+            jax.ShapeDtypeStruct((2048, DP), BF16),
+            jax.ShapeDtypeStruct((8, NEG_OWN, 128), BF16),
+            jax.ShapeDtypeStruct((8, NEG_OWN, 128), BF16),
+            jax.ShapeDtypeStruct((NS, NEG_OWN, 256), BF16),
+            jax.ShapeDtypeStruct((REL, D), BF16),
         ),
         in_specs=[vmem] * 8,
-        out_specs=(vmem,) * 3,
+        out_specs=(anywhere,) * 5,
         scratch_shapes=[pltpu.VMEM(shape, dtype) for shape, dtype in SCRATCH]
         + [
-            pltpu.SemaphoreType.DMA((28,)),
-            pltpu.SemaphoreType.DMA((28,)),
+            pltpu.SemaphoreType.DMA((29,)),
+            pltpu.SemaphoreType.DMA((29,)),
+            pltpu.SemaphoreType.REGULAR((4,)),
+            pltpu.SemaphoreType.DMA((5,)),
         ],
         compiler_params=pltpu.CompilerParams(
             collective_id=0, has_side_effects=True, vmem_limit_bytes=60 * 1024 * 1024
@@ -558,6 +610,33 @@
         send_slots.T,
         dest_rows.T,
     )
+    ent_t, neg_grad, rel_t = pl.pallas_call(
+        finish,
+        out_shape=(
+            jax.ShapeDtypeStruct((D, ENT_DEV), F32),
+            jax.ShapeDtypeStruct((NEG_OWN, D), F32),
+            jax.ShapeDtypeStruct((D, REL), F32),
+        ),
+        in_specs=[anywhere] * 5,
+        out_specs=(anywhere,) * 3,
+        scratch_shapes=[
+            pltpu.VMEM((2048, DP), BF16),
+            pltpu.VMEM((8, NEG_OWN, 128), BF16),
+            pltpu.VMEM((8, NEG_OWN, 128), BF16),
+            pltpu.VMEM((NS, NEG_OWN, 256), BF16),
+            pltpu.VMEM((REL, D), BF16),
+            pltpu.VMEM((2, D, 512), F32),
+            pltpu.VMEM((NEG_OWN, D), F32),
+            pltpu.VMEM((D, REL), F32),
+            pltpu.SemaphoreType.DMA((5,)),
+            pltpu.SemaphoreType.DMA((4,)),
+        ],
+        compiler_params=pltpu.CompilerParams(vmem_limit_bytes=60 * 1024 * 1024),
+        cost_estimate=pl.CostEstimate(
+            flops=2 * 1024 * 2048 * 512, bytes_accessed=6 * 1024 * 1024, transcendentals=0
+        ),
+        name="make_outputs",
+    )(*results)
     return ent_t.T, neg_grad, rel_t.T
 
 

time: 104 us -> 101 us (0.971)
  the two profiles are of different devices: /device:TPU:0 before, /device:TPU:56 now
where the time goes in v1:
time: 101 us
  Pallas kernels  100 us (99%)
    pallas_call x1, Pallas kernels, per_device(): pl.pallas_call(kernel, out_shape=(jax.ShapeDtypeStruct((2048, DP), BF16),...  94.7 us
    pallas_call x1, Pallas kernels, per_device(): pl.pallas_call(finish, out_shape=(jax.ShapeDtypeStruct((D, ENT_DEV), F32)...  5.44 us

profile of v1, /device:TPU:56, one launch (start us, length us, event | category | flops | bytes accessed | tf_op | source)
XLA Modules:
  0.0 101.0 jit_solution(13532048114464131584)
XLA Ops:
  0.6 94.7 %complex_backward.1 = (bf16[2048,512]{1,0:T(8,128)(2,1)}, bf16[8,64,128]{2,1,0:T(8,128)(2,1)}, bf16[8,64,128]{2,1,0:T(8,128)(2,1)}, bf16[16,64,256]{2,1,0:T(8,128)(2,1)}, bf16[512,400]{1,0:T(8,128)(2,1)}) custom-call(bf16[400,512]{1,0:T(8,128)(2,1)} %bitcast.12, bf16[400,512]{1,0:T(8,128)(2,1)} %bitcast.13, s32[1,512]{1,0:T(1,128)} %bitcast.16, ...), custom_call_target="tpu_custom_call" | custom-call | flops 10066329600 | bytes 8388608 | tf_op jit(solution)/shard_map/complex_backward/pallas_call | solution.py:578
  95.4 5.4 %make_outputs.1 = (f32[400,1024]{1,0:T(8,128)}, f32[64,400]{1,0:T(8,128)}, f32[400,512]{1,0:T(8,128)}) custom-call(bf16[2048,512]{1,0:T(8,128)(2,1)} %get-tuple-element.11.arrived_in, bf16[8,64,128]{2,1,0:T(8,128)(2,1)} %get-tuple-element.12.rx2_in, bf16[8,64,128]{2,1,0:T(8,128)(2,1)} %get-tuple-element.13.ry2_in, ...), custom_call_target="tpu_custom_call" | custom-call | flops 2147483648 | bytes 6291456 | tf_op jit(solution)/shard_map/make_outputs/pallas_call | solution.py:613

commit v2 on v1

--- a/solution.py
+++ b/solution.py
@@ -89,7 +89,6 @@
 
     for g in range(8):
         qt[g, D:DP, :] = jnp.zeros((DP - D, EC), BF16)
-    wide[D:, :] = jnp.ones((16, NEG_DEV), BF16)
 
     for i in range(8):
         nbt[i] = neg[:, i * 128 : (i + 1) * 128]
@@ -148,37 +147,41 @@
     def flip(b):
         for i in range(8):
             part = nbt[b * 8 + i]
-            wide[0:D, i * 128 : (i + 1) * 128] = part
+            wide[b, :, i * 128 : (i + 1) * 128] = part
             nb[i * 128 : (i + 1) * 128, 0:D] = part.astype(F32).T.astype(BF16)
 
-    def block(b, two):
-
+    def score(b, two):
         chunks = (2 * two, 2 * two + 1)
         scores = [nn(nb[...], qt[g]) for g in chunks]
         for g, s in zip(chunks, scores):
             m = jnp.max(s, axis=0, keepdims=True)
-            pb = jnp.exp(s - m).astype(BF16)
-            prob[b, :, pl.ds(pl.multiple_of(g * EC, EC), EC)] = pb
-            o = nn(wide[...], pb)
-            l = o[D : D + 1]
-            o = o[0:D]
+            p = jnp.exp(s - m)
+            prob[b, :, pl.ds(pl.multiple_of(g * EC, EC), EC)] = p.astype(BF16)
             mb[b, g, 0:1, :] = m
-            if b == 0:
-                st[g, 0:1, :] = m
-                st[g, 1:2, :] = l
-                st[g, 2:8, :] = jnp.zeros((6, EC), F32)
-                ot[g] = o
-            else:
-                m_old = st[g, 0:1, :]
-                m_new = jnp.maximum(m_old, m)
-                f_old = jnp.exp(m_old - m_new)
-                f_new = jnp.exp(m - m_new)
-                st[g, 0:1, :] = m_new
-                st[g, 1:2, :] = st[g, 1:2, :] * f_old + l * f_new
-                ot[g] = ot[g] * f_old + o * f_new
+            mb[b, g, 1:2, :] = jnp.sum(p, axis=0, keepdims=True)
+
+    def raw_sum(b, g):
+        return nn(wide[b], prob[b, :, pl.ds(pl.multiple_of(g * EC, EC), EC)])
+
+    def raw_first(two):
+        for g in (2 * two, 2 * two + 1):
+            ot[g] = raw_sum(0, g)
+
+    def share(b, g):
+        return sq[g, 1:2, :] * jnp.exp(mb[b, g, 0:1, :] - lt[g, 0:1, :])
+
+    def both_sums(two):
+        for g in (2 * two, 2 * two + 1):
+            ot[g] = ot[g] * share(0, g) + raw_sum(1, g) * share(1, g)
+
+    def merge(out, g, a, b):
+        m = jnp.maximum(a[0:1, :], b[0:1, :])
+        out[g, 0:1, :] = m
+        out[g, 1:2, :] = a[1:2, :] * jnp.exp(a[0:1, :] - m) + b[1:2, :] * jnp.exp(b[0:1, :] - m)
+        out[g, 2:8, :] = jnp.zeros((6, EC), F32)
 
     flip(0)
-    block(0, c)
+    score(0, c)
     pl.semaphore_wait(known.at[0], 3)
     tell(known.at[1], (pair, far))
     wait_bytes(nbt.at[pl.ds(8, 2)], recv.at[GZ_S])
@@ -188,58 +191,43 @@
         rcopy(nbt.at[12 + y], nbt.at[12 + y], send.at[GY_S], recv.at[GY_S], (bucket, x * 4 + yy))
     wait_bytes(qt.at[mine, real], recv.at[Q1_S])
     wait_bytes(sq.at[mine], recv.at[SQ1_S])
-    block(0, oc)
+    score(0, oc)
     pl.semaphore_wait(known.at[1], 2)
     tell(known.at[2], (pair, far))
+    raw_first(c)
     wait_bytes(qt.at[mine, real], recv.at[Q2_S])
     wait_bytes(sq.at[mine], recv.at[SQ2_S])
     rcopy(qt.at[theirs, real], qt.at[theirs, real], send.at[Q3_S], recv.at[Q3_S], partner)
     rcopy(sq.at[theirs], sq.at[theirs], send.at[SQ3_S], recv.at[SQ3_S], partner)
-    block(0, 2 + c)
+    score(0, 2 + c)
+    raw_first(oc)
     wait_bytes(qt.at[mine, real], recv.at[Q3_S])
     wait_bytes(sq.at[mine], recv.at[SQ3_S])
-    block(0, 2 + oc)
+    score(0, 2 + oc)
+    pl.semaphore_wait(known.at[2], 2)
+    tell(known.at[3], (partner,))
     wait_bytes(nbt.at[pl.ds(8, 3)], recv.at[GX_S])
     wait_bytes(nbt.at[pl.ds(8, 3)], recv.at[GY_S])
     flip(1)
-    block(1, 2 + oc)
-    pl.semaphore_wait(known.at[2], 2)
-    tell(known.at[3], (partner,))
-    rcopy(
-        ot.at[pl.ds(4 + 2 * oc, 2)], ot_pair, send.at[O1_S], recv.at[O1_S], partner
-    )
-    block(1, 2 + c)
+
+    def score_far(two, carry):
+        score(1, two)
+        return carry
+
+    lax.fori_loop(0, 4, score_far, 0)
+    pl.semaphore_wait(known.at[3], 1)
+
+    for g in range(8):
+        merge(st, g, mb[0, g], mb[1, g])
+    rcopy(st, st_in, send.at[ST1_S], recv.at[ST1_S], partner)
+    raw_first(2 + oc)
+    wait_bytes(st_in, recv.at[ST1_S])
+    for g in range(8):
+        merge(sc, g, st[g], st_in[g])
     own_half, pair_half = pl.ds(0, 4), pl.ds(4, 4)
-    rcopy(st.at[pair_half], st_in.at[pair_half], send.at[ST1_S], recv.at[ST1_S], partner)
-
-    def merge(g):
-        m_a, m_b = st[g, 0:1, :], st_in[g, 0:1, :]
-        m = jnp.maximum(m_a, m_b)
-        f_a, f_b = jnp.exp(m_a - m), jnp.exp(m_b - m)
-        sc[g, 0:1, :] = m
-        sc[g, 1:2, :] = st[g, 1:2, :] * f_a + st_in[g, 1:2, :] * f_b
-        sc[g, 2:8, :] = jnp.zeros((6, EC), F32)
-        return f_a, f_b
-
-    block(1, oc)
-    pl.semaphore_wait(known.at[3], 1)
-    rcopy(ot.at[pl.ds(2 * oc, 2)], ot_own, send.at[O3_S], recv.at[O3_S], partner)
-    wait_bytes(st_in.at[pair_half], recv.at[ST1_S])
-    wait_bytes(ot_pair, recv.at[O1_S])
-    for g in range(4, 8):
-        merge(g)
-    for j in range(2):
-        f_a, f_b = merge(4 + 2 * c + j)
-        o_sum[j] = (ot[4 + 2 * c + j] * f_a + ot_pair[j] * f_b).astype(BF16)
-    rcopy(o_sum.at[0], o_far.at[0], send.at[O4_S], recv.at[O4_S], pair)
     rcopy(sc.at[pair_half], sc_in.at[own_half], send.at[SC1_S], recv.at[SC1_S], pair)
-    block(1, c)
-    rcopy(st.at[own_half], st_in.at[own_half], send.at[ST2_S], recv.at[ST2_S], partner)
-    wait_bytes(st_in.at[own_half], recv.at[ST2_S])
-    for g in range(4):
-        merge(g)
     rcopy(sc.at[own_half], sc_in.at[pair_half], send.at[SC2_S], recv.at[SC2_S], pair)
-    rcopy(o_sum.at[1], o_far.at[1], send.at[O2_S], recv.at[O2_S], pair)
+    raw_first(2 + c)
     wait_bytes(sc_in.at[own_half], recv.at[SC1_S])
     wait_bytes(sc_in.at[pair_half], recv.at[SC2_S])
     for g in range(8):
@@ -255,8 +243,7 @@
 
     def neg_block(b):
         for g in range(8):
-            scale = sq[g, 1:2, :] * jnp.exp(mb[b, g, 0:1, :] - lt[g, 0:1, :])
-            qs[:, g * EC : (g + 1) * EC] = (qt[g].astype(F32) * scale).astype(BF16)
+            qs[:, g * EC : (g + 1) * EC] = (qt[g].astype(F32) * share(b, g)).astype(BF16)
 
         def rows_of(h, carry):
             rr = pl.ds(pl.multiple_of(h * 512, 512), 512)
@@ -277,20 +264,76 @@
 
     neg_block(1)
     rcopy(gz.at[1], rz1, send.at[Z1_S], recv.at[Z1_S], far)
+    both_sums(2 + oc)
+    rcopy(ot.at[pl.ds(4 + 2 * oc, 2)], ot_pair, send.at[O1_S], recv.at[O1_S], partner)
+    both_sums(2 + c)
+    wait_bytes(ot_pair, recv.at[O1_S])
+    for j in range(2):
+        o_sum[j] = (ot[4 + 2 * c + j] + ot_pair[j]).astype(BF16)
+    rcopy(o_sum, o_far, send.at[O2_S], recv.at[O2_S], pair)
+    neg_block(0)
+    both_sums(oc)
+    rcopy(ot.at[pl.ds(2 * oc, 2)], ot_own, send.at[O3_S], recv.at[O3_S], partner)
+    both_sums(c)
+
+    my_rows = pl.ds(pl.multiple_of(shard * NEG_OWN, NEG_OWN), NEG_OWN)
+    wait_bytes(rx1.at[pl.ds(0, 3)], recv.at[X1_S])
+    for b in range(2):
+        total = gx[b, x].astype(F32)
+        for i in range(1, 4):
+            total = total + rx1[lax.rem(x + i, 4), b].astype(F32)
+        ax[b] = total.astype(BF16)
+    for i in range(4):
+        yy = lax.rem(y + i, 4)
+        rows = pl.ds(pl.multiple_of(yy * NEG_OWN, NEG_OWN), NEG_OWN)
+        if i:
+            rcopy(ax.at[0, rows], rx2.at[y], send.at[X2_S], recv.at[X2_S], (bucket, x * 4 + yy))
+        else:
+            rx2[y] = ax[0, rows, :]
+        rcopy(
+            ax.at[1, rows], rx2.at[4 + y], send.at[X2_S], recv.at[X2_S], (z_far * 2 + c, x * 4 + yy)
+        )
+    wait_bytes(ry1.at[pl.ds(0, 3)], recv.at[Y1_S])
+    for b in range(2):
+        total = gy[b, y].astype(F32)
+        for i in range(1, 4):
+            total = total + ry1[lax.rem(y + i, 4), b].astype(F32)
+        ay[b] = total.astype(BF16)
+    for i in range(4):
+        xx = lax.rem(x + i, 4)
+        if i:
+            rcopy(ay.at[0, xx], ry2.at[x], send.at[Y2_S], recv.at[Y2_S], (bucket, xx * 4 + y))
+        else:
+            ry2[x] = ay[0, x]
+        rcopy(
+            ay.at[1, xx], ry2.at[4 + x], send.at[Y2_S], recv.at[Y2_S], (z_far * 2 + c, xx * 4 + y)
+        )
+    wait_bytes(rz1, recv.at[Z1_S])
+
+    def sum_z(r, carry):
+        rr = pl.ds(pl.multiple_of(r * 256, 256), 256)
+        total = gz[0, :, rr].astype(F32) + rz1[:, rr].astype(F32)
+        wide_sum = jnp.concatenate([total, jnp.zeros((256 - (D - 256), 256), F32)], axis=0)
+        az[rr, :] = wide_sum.T.astype(BF16)
+        return carry
+
+    lax.fori_loop(0, 4, sum_z, 0)
+    for j in range(1, NS):
+        ss = lax.rem(shard + j, NS)
+        rows = az.at[pl.ds(pl.multiple_of(ss * NEG_OWN, NEG_OWN), NEG_OWN)]
+        rcopy(rows, rz2.at[shard], send.at[Z2_S], recv.at[Z2_S], (bucket, ss))
+    rz2[shard] = az[my_rows, :]
+
     wait_bytes(ot_own, recv.at[O3_S])
-    wait_bytes(o_far.at[0], recv.at[O4_S])
-    wait_bytes(o_far.at[1], recv.at[O2_S])
+    wait_bytes(o_far, recv.at[O2_S])
     ends[D:DP, :] = jnp.zeros((DP - D, 2 * E_DEV), BF16)
     for j in range(2):
         cols = slice(j * EC, (j + 1) * EC)
         tail_cols = slice(E_DEV + j * EC, E_DEV + (j + 1) * EC)
         g = 2 * c + j
-        pos, w, ltot = sq[g, 0:1, :], sq[g, 1:2, :], lt[g, 0:1, :]
-        pos_coef = w * (jnp.exp(pos - ltot) - 1.0)
-        own = w * jnp.exp(st[g, 0:1, :] - ltot)
-        other = w * jnp.exp(st_in[g, 0:1, :] - ltot)
-        away = w * jnp.exp(sc_in[g, 0:1, :] - ltot)
-        grad = pos_coef * tts[j] + ot[g] * own + ot_own[j] * other + o_far[j].astype(F32) * away
+        pos, ltot = sq[g, 0:1, :], lt[g, 0:1, :]
+        pos_coef = sq[g, 1:2, :] * (jnp.exp(pos - ltot) - 1.0)
+        grad = pos_coef * tts[j] + ot[g] + ot_own[j] + o_far[j].astype(F32)
         gre, gim = grad[:HALF], grad[HALF:]
         rre, rim = rts[j, :HALF, :], rts[j, HALF:, :]
         hre, him = hts[j, :HALF, :], hts[j, HALF:, :]
@@ -341,12 +384,7 @@
         rp.at[pl.ds(pl.multiple_of(oc * 256, 256), 256)], rp_in, send.at[RC_S], recv.at[RC_S], partner
     )
 
-    def pack_other(k, carry):
-        pack(k, False)
-        return carry
-
     pack(0, True)
-    lax.fori_loop(1, 2, pack_other, 0)
 
     wait_bytes(rp_in, recv.at[RC_S])
     r1b[...] = (rp[pl.ds(pl.multiple_of(c * 256, 256), 256), :] + rp_in[...]).astype(BF16)
@@ -355,9 +393,8 @@
         rows = r1b.at[pl.ds(pl.multiple_of(ss * 16, 16), 16)]
         rcopy(rows, r2in.at[shard], send.at[R2_S], recv.at[R2_S], (bucket, ss))
     r2in[shard] = r1b[pl.ds(pl.multiple_of(shard * 16, 16), 16), :]
-    neg_block(0)
-    lax.fori_loop(2, NB // 2, pack_other, 0)
-
+
+    pack(1, False)
 
     wait_bytes(r2in.at[pl.ds(0, NS - 1)], recv.at[R2_S])
     r2 = r2in[0].astype(F32)
@@ -368,23 +405,9 @@
         zz = lax.rem(z + k, NZ)
         rcopy(r2all.at[z], r2all.at[z], send.at[R3_S], recv.at[R3_S], (zz * 2 + c, shard))
 
-    my_rows = pl.ds(pl.multiple_of(shard * NEG_OWN, NEG_OWN), NEG_OWN)
-    wait_bytes(rx1.at[pl.ds(0, 3)], recv.at[X1_S])
-    for b in range(2):
-        total = gx[b, x].astype(F32)
-        for i in range(1, 4):
-            total = total + rx1[lax.rem(x + i, 4), b].astype(F32)
-        ax[b] = total.astype(BF16)
-    for i in range(4):
-        yy = lax.rem(y + i, 4)
-        rows = pl.ds(pl.multiple_of(yy * NEG_OWN, NEG_OWN), NEG_OWN)
-        if i:
-            rcopy(ax.at[0, rows], rx2.at[y], send.at[X2_S], recv.at[X2_S], (bucket, x * 4 + yy))
-        else:
-            rx2[y] = ax[0, rows, :]
-        rcopy(
-            ax.at[1, rows], rx2.at[4 + y], send.at[X2_S], recv.at[X2_S], (z_far * 2 + c, x * 4 + yy)
-        )
+
+    pack(2, False)
+
     wait_bytes(r2all.at[pl.ds(0, 3)], recv.at[R3_S])
     rel_row = pl.ds(pl.multiple_of(c * 256 + shard * 16, 16), 16)
     rfin[rel_row, :] = (((r2all[0] + r2all[1]) + r2all[2]) + r2all[3]).astype(BF16)
@@ -392,36 +415,7 @@
         ss = lax.rem(shard + j, NS)
         rcopy(rfin.at[rel_row], rfin.at[rel_row], send.at[R4_S], recv.at[R4_S], (bucket, ss))
 
-    wait_bytes(ry1.at[pl.ds(0, 3)], recv.at[Y1_S])
-    for b in range(2):
-        total = gy[b, y].astype(F32)
-        for i in range(1, 4):
-            total = total + ry1[lax.rem(y + i, 4), b].astype(F32)
-        ay[b] = total.astype(BF16)
-    for i in range(4):
-        xx = lax.rem(x + i, 4)
-        if i:
-            rcopy(ay.at[0, xx], ry2.at[x], send.at[Y2_S], recv.at[Y2_S], (bucket, xx * 4 + y))
-        else:
-            ry2[x] = ay[0, x]
-        rcopy(
-            ay.at[1, xx], ry2.at[4 + x], send.at[Y2_S], recv.at[Y2_S], (z_far * 2 + c, xx * 4 + y)
-        )
-    wait_bytes(rz1, recv.at[Z1_S])
-
-    def sum_z(r, carry):
-        rr = pl.ds(pl.multiple_of(r * 256, 256), 256)
-        total = gz[0, :, rr].astype(F32) + rz1[:, rr].astype(F32)
-        wide_sum = jnp.concatenate([total, jnp.zeros((256 - (D - 256), 256), F32)], axis=0)
-        az[rr, :] = wide_sum.T.astype(BF16)
-        return carry
-
-    lax.fori_loop(0, 4, sum_z, 0)
-    for j in range(1, NS):
-        ss = lax.rem(shard + j, NS)
-        rows = az.at[pl.ds(pl.multiple_of(ss * NEG_OWN, NEG_OWN), NEG_OWN)]
-        rcopy(rows, rz2.at[shard], send.at[Z2_S], recv.at[Z2_S], (bucket, ss))
-    rz2[shard] = az[my_rows, :]
+    pack(3, False)
 
     def give(src, dst, sem):
         pltpu.make_async_copy(src, dst, sem).start()
@@ -447,11 +441,11 @@
         wait_bytes(qt.at[mine, real], send.at[number])
     for number in (SQ1_S, SQ2_S, SQ3_S):
         wait_bytes(sq.at[mine], send.at[number])
-    for number in (ST1_S, ST2_S, SC1_S, SC2_S):
+    wait_bytes(st, send.at[ST1_S])
+    for number in (SC1_S, SC2_S):
         wait_bytes(st.at[own_half], send.at[number])
     wait_bytes(ot_pair, send.at[O1_S])
-    wait_bytes(o_far.at[0], send.at[O4_S])
-    wait_bytes(o_far.at[1], send.at[O2_S])
+    wait_bytes(o_far, send.at[O2_S])
     wait_bytes(ot_own, send.at[O3_S])
     wait_bytes(arrived.at[pl.ds(0, 2048 - SLOT)], send.at[ENT_S])
     wait_bytes(rp_in, send.at[RC_S])
@@ -522,7 +516,7 @@
 
 SCRATCH = [
     ((16, D, 128), BF16),
-    ((D + 16, NEG_DEV), BF16),
+    ((2, D, NEG_DEV), BF16),
     ((NEG_DEV, DP), BF16),
     ((2, NEG_DEV, 8 * EC), BF16),
     ((8, DP, EC), BF16),

time: 101 us -> 106 us (1.050)
  the two profiles are of different devices: /device:TPU:56 before, /device:TPU:0 now
where the time goes in v2:
time: 106 us; the launch traced here: 105 us
  Pallas kernels  104 us (98%)
    pallas_call x1, Pallas kernels, per_device(): pl.pallas_call(kernel, out_shape=(jax.ShapeDtypeStruct((2048, DP), BF16),...  98.6 us
    pallas_call x1, Pallas kernels, per_device(): pl.pallas_call(finish, out_shape=(jax.ShapeDtypeStruct((D, ENT_DEV), F32)...  5.44 us

profile of v2, /device:TPU:0, one launch (start us, length us, event | category | flops | bytes accessed | tf_op | source)
XLA Modules:
  0.0 104.8 jit_solution(8509349224538964739)
XLA Ops:
  0.6 98.6 %complex_backward.1 = (bf16[2048,512]{1,0:T(8,128)(2,1)}, bf16[8,64,128]{2,1,0:T(8,128)(2,1)}, bf16[8,64,128]{2,1,0:T(8,128)(2,1)}, bf16[16,64,256]{2,1,0:T(8,128)(2,1)}, bf16[512,400]{1,0:T(8,128)(2,1)}) custom-call(bf16[400,512]{1,0:T(8,128)(2,1)} %bitcast.12, bf16[400,512]{1,0:T(8,128)(2,1)} %bitcast.13, s32[1,512]{1,0:T(1,128)} %bitcast.16, ...), custom_call_target="tpu_custom_call" | custom-call | flops 10066329600 | bytes 8388608 | tf_op jit(solution)/shard_map/complex_backward/pallas_call | solution.py:572
  99.2 5.4 %make_outputs.1 = (f32[400,1024]{1,0:T(8,128)}, f32[64,400]{1,0:T(8,128)}, f32[400,512]{1,0:T(8,128)}) custom-call(bf16[2048,512]{1,0:T(8,128)(2,1)} %get-tuple-element.11.arrived_in, bf16[8,64,128]{2,1,0:T(8,128)(2,1)} %get-tuple-element.12.rx2_in, bf16[8,64,128]{2,1,0:T(8,128)(2,1)} %get-tuple-element.13.ry2_in, ...), custom_call_target="tpu_custom_call" | custom-call | flops 2147483648 | bytes 6291456 | tf_op jit(solution)/shard_map/make_outputs/pallas_call | solution.py:607

commit v3 on v1

--- a/solution.py
+++ b/solution.py
@@ -26,7 +26,8 @@
 BF16 = jnp.bfloat16
 
 (Q1_S, SQ1_S, Q2_S, SQ2_S, Q3_S, SQ3_S, ST1_S, O1_S, SC1_S, O2_S, ST2_S, O3_S, SC2_S,
- RC_S, R2_S, R3_S, R4_S, R5_S, ENT_S, Z1_S, X1_S, Y1_S, Z2_S, X2_S, Y2_S, GZ_S, GX_S, GY_S, O4_S) = range(29)
+ RC_S, R2_S, R3_S, R4_S, R5_S, ENT_S, Z1_S, X1_S, Y1_S, Z2_S, X2_S, Y2_S, GZ_S, GX_S, GY_S, O4_S,
+ PX_S, PY_S) = range(31)
 
 
 def nt(a, b):
@@ -51,19 +52,18 @@
 
 def kernel(
     head, tail, ids, rel, wts, neg, slots, drows,
-    arrived_out, rx2_out, ry2_out, rz2_out, rel_sum_out,
+    main_out, last_out, far_main_out, far_last_out, rx2_out, ry2_out, rz2_out, rel_sum_out,
     nbt, wide, nb, prob, qt, sq, hts, tts, rts, mb, st, st_in, sc, sc_in,
     ot, ot_pair, ot_own, o_sum, o_far, lt, qs, ends, rt_hi, rt_lo,
-    packed, arrived, slot_col, dest_col,
+    packed, arrived, far_main, far_last, slot_col, dest_col,
     gz, gx, gy, rz1, rx1, ry1, az, ax, ay, rz2, rx2, ry2,
     rp, rp_in, r1b, r2in, r2all, rfin,
-    send, recv, known, out_sem,
+    send, recv, known, out_sem, ent_recv,
 ):
     bucket, shard = lax.axis_index("bucket"), lax.axis_index("shard")
     z, c = bucket // 2, bucket % 2
     x, y = shard // 4, shard % 4
     oc = 1 - c
-    me = bucket * NS + shard
     partner = (z * 2 + oc, shard)
     pair = ((z + 1 - 2 * (z % 2)) * 2 + c, shard)
     z_far = 3 - z
@@ -294,42 +294,52 @@
         gre, gim = grad[:HALF], grad[HALF:]
         rre, rim = rts[j, :HALF, :], rts[j, HALF:, :]
         hre, him = hts[j, :HALF, :], hts[j, HALF:, :]
-        ends[0:D, cols] = jnp.concatenate(
+        head_grad = jnp.concatenate(
             [gre * rre + gim * rim, gim * rre - gre * rim], axis=0
         ).astype(BF16)
-        ends[0:D, tail_cols] = (pos_coef * qt[g, 0:D, :].astype(F32)).astype(BF16)
+        tail_grad = (pos_coef * qt[g, 0:D, :].astype(F32)).astype(BF16)
+        for part, where_to in ((head_grad, cols), (tail_grad, tail_cols)):
+            ends[0:D, where_to] = part
+            ends[416:432, where_to] = part[384:D]
         term = jnp.concatenate([gre * hre + gim * him, gim * hre - gre * him], axis=0)
         hi = term.astype(BF16)
         rt_hi[:, cols] = hi
         rt_lo[:, cols] = (term - hi.astype(F32)).astype(BF16)
 
-    my_slots = pl.ds(pl.multiple_of(me * SLOT, SLOT), SLOT)
+    src_chip = z * NS + shard
 
     def pack(k, first):
+        zz = lax.rem(z + k, NZ)
+        chips = pl.ds(pl.multiple_of(zz * NS, NS), NS)
         sel = []
-        for u in range(2):
-            sc_b = slot_col[lax.rem(bucket + 2 * k + u, NB)]
+        for d in range(2):
+            sc_b = slot_col[zz * 2 + d]
             sel.append(jnp.concatenate(
                 [hot_where(sc_b == (iota((256, 128), 1) + 128 * t).astype(F32)) for t in range(8)],
                 axis=1,
             ))
         rows = nt(jnp.concatenate(sel, axis=0), ends[...])
-        for u in range(2):
-            bb = lax.rem(bucket + 2 * k + u, NB)
-            part = rows[u * 256 : (u + 1) * 256]
-            dc = dest_col[bb]
+        lane = iota((256, 128), 1)
+        last = []
+        for d in range(2):
+            part = rows[d * 256 : (d + 1) * 256]
+            for t in range(3):
+                first_row = (d * 3 + t) * SLOT
+                tile = part[:, t * 128 : (t + 1) * 128].astype(BF16).reshape(NS, SLOT, 128)
+                packed[chips, first_row : first_row + SLOT, :] = tile
+            dc = dest_col[zz * 2 + d]
             high = jnp.floor(dc * (1.0 / 32.0))
-            lane = iota((256, 128), 1)
-            code = jnp.where(lane == 16, high, jnp.where(lane == 17, dc - 32.0 * high, 0.0))
-            packed[bb, :, 0:384] = part[:, 0:384].astype(BF16)
-            packed[bb, :, 384:512] = (part[:, 384:512] + code).astype(BF16)
-            for j in range(NS):
-                ss = lax.rem(shard + j, NS)
-                src = packed.at[bb, pl.ds(pl.multiple_of(ss * SLOT, SLOT), SLOT)]
-                if first and u == 0 and j == 0:
-                    pltpu.make_async_copy(src, arrived.at[my_slots], recv.at[ENT_S]).start()
-                else:
-                    rcopy(src, arrived.at[my_slots], send.at[ENT_S], recv.at[ENT_S], (bb, ss))
+            code = jnp.where(lane == 32 * d + 16, high, jnp.where(lane == 32 * d + 17, dc - 32.0 * high, 0.0))
+            last.append(part[:, 384:512] + code)
+        tile = jnp.where(lane < 32, last[0], last[1]).astype(BF16).reshape(NS, SLOT, 128)
+        packed[chips, 96:112, :] = tile
+        for j in range(NS):
+            ss = lax.rem(shard + j, NS)
+            src = packed.at[zz * NS + ss]
+            if first and j == 0:
+                pltpu.make_async_copy(src, arrived.at[src_chip], ent_recv.at[k]).start()
+            else:
+                rcopy(src, arrived.at[src_chip], send.at[ENT_S], ent_recv.at[k], (zz * 2 + c, ss))
 
     def rel_chunk(r, carry):
         hot = hot_where(iota((128, E_DEV), 0) + r * 128 == ids[...])
@@ -426,8 +436,14 @@
     def give(src, dst, sem):
         pltpu.make_async_copy(src, dst, sem).start()
 
-    wait_bytes(arrived, recv.at[ENT_S])
-    give(arrived, arrived_out, out_sem.at[0])
+    other_rows, last_rows = pl.ds(pl.multiple_of(oc * 48, 16), 48), pl.ds(96, SLOT)
+    for k in range(NZ):
+        chips = pl.ds(pl.multiple_of(lax.rem(z + NZ - k, NZ) * NS, NS), NS)
+        wait_bytes(arrived.at[chips], ent_recv.at[k])
+        rcopy(arrived.at[chips, other_rows], far_main.at[chips], send.at[PX_S], recv.at[PX_S], partner)
+        rcopy(arrived.at[chips, last_rows], far_last.at[chips], send.at[PY_S], recv.at[PY_S], partner)
+    give(arrived.at[:, pl.ds(pl.multiple_of(c * 48, 16), 48)], main_out, out_sem.at[0])
+    give(arrived.at[:, last_rows], last_out, out_sem.at[5])
     wait_bytes(rfin.at[pl.ds(0, 240)], recv.at[R4_S])
     half_rel = rfin.at[pl.ds(pl.multiple_of(c * 256, 256), 256)]
     rcopy(half_rel, half_rel, send.at[R5_S], recv.at[R5_S], partner)
@@ -439,6 +455,10 @@
     give(rz2, rz2_out, out_sem.at[3])
     wait_bytes(half_rel, recv.at[R5_S])
     give(rfin, rel_sum_out, out_sem.at[4])
+    wait_bytes(far_main, recv.at[PX_S])
+    give(far_main, far_main_out, out_sem.at[6])
+    wait_bytes(far_last, recv.at[PY_S])
+    give(far_last, far_last_out, out_sem.at[7])
 
     wait_bytes(nbt.at[pl.ds(0, 2)], send.at[GZ_S])
     wait_bytes(nbt.at[pl.ds(0, 3)], send.at[GX_S])
@@ -453,7 +473,9 @@
     wait_bytes(o_far.at[0], send.at[O4_S])
     wait_bytes(o_far.at[1], send.at[O2_S])
     wait_bytes(ot_own, send.at[O3_S])
-    wait_bytes(arrived.at[pl.ds(0, 2048 - SLOT)], send.at[ENT_S])
+    wait_bytes(arrived.at[pl.ds(0, 63)], send.at[ENT_S])
+    wait_bytes(far_main, send.at[PX_S])
+    wait_bytes(far_last, send.at[PY_S])
     wait_bytes(rp_in, send.at[RC_S])
     wait_bytes(r2in.at[pl.ds(0, NS - 1)], send.at[R2_S])
     wait_bytes(r2all.at[pl.ds(0, 3)], send.at[R3_S])
@@ -465,7 +487,10 @@
     wait_bytes(rx2.at[pl.ds(0, 7)], send.at[X2_S])
     wait_bytes(ry2.at[pl.ds(0, 7)], send.at[Y2_S])
     wait_bytes(rz2.at[pl.ds(0, NS - 1)], send.at[Z2_S])
-    wait_bytes(arrived, out_sem.at[0])
+    for number in (0, 6):
+        wait_bytes(far_main, out_sem.at[number])
+    for number in (5, 7):
+        wait_bytes(far_last, out_sem.at[number])
     wait_bytes(rx2, out_sem.at[1])
     wait_bytes(ry2, out_sem.at[2])
     wait_bytes(rz2, out_sem.at[3])
@@ -473,13 +498,15 @@
 
 
 def finish(
-    arrived_in, rx2_in, ry2_in, rz2_in, rel_in, ent_out, neg_out, rel_out,
-    arrived, rx2, ry2, rz2, rel_sum, ent, neg_sum, rel_t, in_sem, out_sem,
+    main_in, last_in, far_main_in, far_last_in, rx2_in, ry2_in, rz2_in, rel_in,
+    ent_out, neg_out, rel_out,
+    main, last, far_main, far_last, rx2, ry2, rz2, rel_sum, ent, neg_sum, rel_t, in_sem, out_sem,
 ):
     loads = [
         pltpu.make_async_copy(src, dst, in_sem.at[i])
         for i, (src, dst) in enumerate((
-            (rel_in, rel_sum), (arrived_in, arrived), (rx2_in, rx2), (ry2_in, ry2), (rz2_in, rz2)
+            (rel_in, rel_sum), (last_in, last), (far_last_in, far_last), (main_in, main),
+            (far_main_in, far_main), (rx2_in, rx2), (ry2_in, ry2), (rz2_in, rz2),
         ))
     ]
     for load in loads:
@@ -492,13 +519,23 @@
     stores = [pltpu.make_async_copy(rel_t, rel_out, out_sem.at[0])]
     stores[0].start()
 
-    loads[1].wait()
-    lane = iota((8, 128), 1)
-    unit = jnp.where(lane == D - 384, 32.0, jnp.where(lane == D - 383, 1.0, 0.0)).astype(BF16)
-    row_ids = nt(unit, arrived[:, 384:DP])[0:1, :]
+    c = lax.axis_index("bucket") % 2
+    lane = iota((8, 128), 1) - 32 * c
+    unit = jnp.where(lane == 16, 32.0, jnp.where(lane == 17, 1.0, 0.0)).astype(BF16)
+    for load in loads[1:5]:
+        load.wait()
+    slots, row_ids = [], []
+    for tiles, tail in ((main, last), (far_main, far_last)):
+        tail_rows = tail[...].reshape(1024, 128)
+        columns = [tiles[:, t * SLOT : (t + 1) * SLOT, :].reshape(1024, 128) for t in range(3)]
+        slots.append(jnp.concatenate(columns + [tail_rows], axis=1))
+        row_ids.append(nt(unit, tail_rows)[0:1, :])
     for r in range(2):
-        hot = hot_where((iota((512, 2048), 0) + r * 512).astype(F32) == row_ids)
-        ent[r] = nn(hot, arrived[...]).T[0:D]
+        numbers = (iota((512, 1024), 0) + r * 512).astype(F32)
+        got = nn(hot_where(numbers == row_ids[0]), slots[0]) + nn(hot_where(numbers == row_ids[1]), slots[1])
+        turned = got.T
+        ent[r, 0:384] = turned[0:384]
+        ent[r, 384:D] = jnp.where(c == 0, turned[384:400], turned[416:432])
         store = pltpu.make_async_copy(ent.at[r], ent_out.at[:, pl.ds(r * 512, 512)], out_sem.at[1 + r])
         store.start()
         stores.append(store)
@@ -509,7 +546,7 @@
             total = total + ref[i].astype(F32)
         return total
 
-    for load in loads[2:]:
+    for load in loads[5:]:
         load.wait()
     neg_sum[:, 0:128] = sum_all(rx2)
     neg_sum[:, 128:256] = sum_all(ry2)
@@ -545,8 +582,10 @@
     ((DP, 2 * E_DEV), BF16),
     ((D, E_DEV), BF16),
     ((D, E_DEV), BF16),
-    ((NB, 256, DP), BF16),
-    ((2048, DP), BF16),
+    ((NZ * NS, 112, 128), BF16),
+    ((NZ * NS, 112, 128), BF16),
+    ((NZ * NS, 48, 128), BF16),
+    ((NZ * NS, SLOT, 128), BF16),
     ((NB, 256, 128), F32),
     ((NB, 256, 128), F32),
     ((2, D - 256, NEG_DEV), BF16),
@@ -578,20 +617,24 @@
     results = pl.pallas_call(
         kernel,
         out_shape=(
-            jax.ShapeDtypeStruct((2048, DP), BF16),
+            jax.ShapeDtypeStruct((NZ * NS, 48, 128), BF16),
+            jax.ShapeDtypeStruct((NZ * NS, SLOT, 128), BF16),
+            jax.ShapeDtypeStruct((NZ * NS, 48, 128), BF16),
+            jax.ShapeDtypeStruct((NZ * NS, SLOT, 128), BF16),
             jax.ShapeDtypeStruct((8, NEG_OWN, 128), BF16),
             jax.ShapeDtypeStruct((8, NEG_OWN, 128), BF16),
             jax.ShapeDtypeStruct((NS, NEG_OWN, 256), BF16),
             jax.ShapeDtypeStruct((REL, D), BF16),
         ),
         in_specs=[vmem] * 8,
-        out_specs=(anywhere,) * 5,
+        out_specs=(anywhere,) * 8,
         scratch_shapes=[pltpu.VMEM(shape, dtype) for shape, dtype in SCRATCH]
         + [
-            pltpu.SemaphoreType.DMA((29,)),
-            pltpu.SemaphoreType.DMA((29,)),
+            pltpu.SemaphoreType.DMA((31,)),
+            pltpu.SemaphoreType.DMA((31,)),
             pltpu.SemaphoreType.REGULAR((4,)),
-            pltpu.SemaphoreType.DMA((5,)),
+            pltpu.SemaphoreType.DMA((8,)),
+            pltpu.SemaphoreType.DMA((NZ,)),
         ],
         compiler_params=pltpu.CompilerParams(
             collective_id=0, has_side_effects=True, vmem_limit_bytes=60 * 1024 * 1024
@@ -617,10 +660,13 @@
             jax.ShapeDtypeStruct((NEG_OWN, D), F32),
             jax.ShapeDtypeStruct((D, REL), F32),
         ),
-        in_specs=[anywhere] * 5,
+        in_specs=[anywhere] * 8,
         out_specs=(anywhere,) * 3,
         scratch_shapes=[
-            pltpu.VMEM((2048, DP), BF16),
+            pltpu.VMEM((NZ * NS, 48, 128), BF16),
+            pltpu.VMEM((NZ * NS, SLOT, 128), BF16),
+            pltpu.VMEM((NZ * NS, 48, 128), BF16),
+            pltpu.VMEM((NZ * NS, SLOT, 128), BF16),
             pltpu.VMEM((8, NEG_OWN, 128), BF16),
             pltpu.VMEM((8, NEG_OWN, 128), BF16),
             pltpu.VMEM((NS, NEG_OWN, 256), BF16),
@@ -628,7 +674,7 @@
             pltpu.VMEM((2, D, 512), F32),
             pltpu.VMEM((NEG_OWN, D), F32),
             pltpu.VMEM((D, REL), F32),
-            pltpu.SemaphoreType.DMA((5,)),
+            pltpu.SemaphoreType.DMA((8,)),
             pltpu.SemaphoreType.DMA((4,)),
         ],
         compiler_params=pltpu.CompilerParams(vmem_limit_bytes=60 * 1024 * 1024),

time: 101 us -> 102 us (level)
  the two profiles are of different devices: /device:TPU:56 before, /device:TPU:32 now
where the time goes in v3:
time: 102 us; the launch traced here: 101 us
  Pallas kernels  101 us (99%)
    pallas_call x1, Pallas kernels, per_device(): pl.pallas_call(kernel, out_shape=(jax.ShapeDtypeStruct((NZ * NS, 48, 128)...  95.2 us
    pallas_call x1, Pallas kernels, per_device(): pl.pallas_call(finish, out_shape=(jax.ShapeDtypeStruct((D, ENT_DEV), F32)...  5.44 us

profile of v3, /device:TPU:32, one launch (start us, length us, event | category | flops | bytes accessed | tf_op | source)
XLA Modules:
  0.0 101.5 jit_solution(3224796000108267776)
XLA Ops:
  0.6 95.2 %complex_backward.1 = (bf16[64,48,128]{2,1,0:T(8,128)(2,1)}, bf16[64,16,128]{2,1,0:T(8,128)(2,1)}, bf16[64,48,128]{2,1,0:T(8,128)(2,1)}, bf16[64,16,128]{2,1,0:T...) custom-call(bf16[400,512]{1,0:T(8,128)(2,1)} %bitcast.12, ...), custom_call_target="tpu_custom_call" | custom-call | flops 10066329600 | bytes 8388608 | tf_op jit(solution)/shard_map/complex_backward/pallas_call | solution.py:617
  95.9 5.4 %make_outputs.1 = (f32[400,1024]{1,0:T(8,128)}, f32[64,400]{1,0:T(8,128)}, f32[400,512]{1,0:T(8,128)}) custom-call(bf16[64,48,128]{2,1,0:T(8,128)(2,1)} %get-tuple-element.14.main_in, bf16[64,16,128]{2,1,0:T(8,128)(2,1)} %get-tuple-element.15.last_in, bf16[64,48,128]{2,1,0:T(8,128)(2,1)} %get-tuple-element.16.far_main_in, ...), custom_call_target="tpu_custom_call" | custom-call | flops 2147483648 | bytes 6291456 | tf_op jit(solution)/shard_map/make_outputs/pallas_call | solution.py:656

commit v4 on v3

--- a/solution.py
+++ b/solution.py
@@ -25,9 +25,19 @@
 F32 = jnp.float32
 BF16 = jnp.bfloat16
 
+FAR_OFFSETS = [
+    (dx, dy, dz) for dz in range(4) for dx in range(4) for dy in range(4) if 2 in (dx, dy, dz)
+]
+FORWARDED = [(dx, dy, dz) for dx, dy, dz in FAR_OFFSETS if (dy + dz) % 4 < 2]
+
+
+def steps_back(offset):
+    return tuple(int(d == 2) for d in offset)
+
+
 (Q1_S, SQ1_S, Q2_S, SQ2_S, Q3_S, SQ3_S, ST1_S, O1_S, SC1_S, O2_S, ST2_S, O3_S, SC2_S,
  RC_S, R2_S, R3_S, R4_S, R5_S, ENT_S, Z1_S, X1_S, Y1_S, Z2_S, X2_S, Y2_S, GZ_S, GX_S, GY_S, O4_S,
- PX_S, PY_S) = range(31)
+ PX_S, PY_S, FW_S) = range(32)
 
 
 def nt(a, b):
@@ -55,7 +65,7 @@
     main_out, last_out, far_main_out, far_last_out, rx2_out, ry2_out, rz2_out, rel_sum_out,
     nbt, wide, nb, prob, qt, sq, hts, tts, rts, mb, st, st_in, sc, sc_in,
     ot, ot_pair, ot_own, o_sum, o_far, lt, qs, ends, rt_hi, rt_lo,
-    packed, arrived, far_main, far_last, slot_col, dest_col,
+    packed, arrived, passing, far_main, far_last, slot_col, dest_col,
     gz, gx, gy, rz1, rx1, ry1, az, ax, ay, rz2, rx2, ry2,
     rp, rp_in, r1b, r2in, r2all, rfin,
     send, recv, known, out_sem, ent_recv,
@@ -308,7 +318,11 @@
 
     src_chip = z * NS + shard
 
-    def pack(k, first):
+    def chip_at(offset):
+        dx, dy, dz = offset
+        return (z + dz + 4) % 4, (x + dx + 4) % 4 * 4 + (y + dy + 4) % 4
+
+    def pack(k):
         zz = lax.rem(z + k, NZ)
         chips = pl.ds(pl.multiple_of(zz * NS, NS), NS)
         sel = []
@@ -333,13 +347,31 @@
             last.append(part[:, 384:512] + code)
         tile = jnp.where(lane < 32, last[0], last[1]).astype(BF16).reshape(NS, SLOT, 128)
         packed[chips, 96:112, :] = tile
-        for j in range(NS):
-            ss = lax.rem(shard + j, NS)
+        offsets = [(dx, dy, k) for dx in range(4) for dy in range(4)]
+        for offset in sorted(offsets, key=lambda o: o not in FORWARDED):
+            ss = chip_at(offset)[1]
             src = packed.at[zz * NS + ss]
-            if first and j == 0:
+            if offset == (0, 0, 0):
                 pltpu.make_async_copy(src, arrived.at[src_chip], ent_recv.at[k]).start()
+            elif offset in FORWARDED:
+                bx, by, bz = steps_back(offset)
+                way_z, way_shard = chip_at((-bx, -by, -bz))
+                number = FORWARDED.index(offset)
+                rcopy(src, passing.at[number], send.at[ENT_S], recv.at[FW_S], (way_z * 2 + c, way_shard))
             else:
                 rcopy(src, arrived.at[src_chip], send.at[ENT_S], ent_recv.at[k], (zz * 2 + c, ss))
+
+    def pass_on():
+        wait_bytes(passing, recv.at[FW_S])
+        for number, offset in enumerate(FORWARDED):
+            back = steps_back(offset)
+            from_z, from_shard = chip_at(back)
+            to_z, to_shard = chip_at(tuple(d + b for d, b in zip(offset, back)))
+            rcopy(
+                passing.at[number], arrived.at[from_z * NS + from_shard], send.at[FW_S],
+                ent_recv.at[offset[2]], (to_z * 2 + c, to_shard),
+            )
+
 
     def rel_chunk(r, carry):
         hot = hot_where(iota((128, E_DEV), 0) + r * 128 == ids[...])
@@ -351,12 +383,8 @@
         rp.at[pl.ds(pl.multiple_of(oc * 256, 256), 256)], rp_in, send.at[RC_S], recv.at[RC_S], partner
     )
 
-    def pack_other(k, carry):
-        pack(k, False)
-        return carry
-
-    pack(0, True)
-    lax.fori_loop(1, 2, pack_other, 0)
+    pack(0)
+    pack(1)
 
     wait_bytes(rp_in, recv.at[RC_S])
     r1b[...] = (rp[pl.ds(pl.multiple_of(c * 256, 256), 256), :] + rp_in[...]).astype(BF16)
@@ -366,7 +394,8 @@
         rcopy(rows, r2in.at[shard], send.at[R2_S], recv.at[R2_S], (bucket, ss))
     r2in[shard] = r1b[pl.ds(pl.multiple_of(shard * 16, 16), 16), :]
     neg_block(0)
-    lax.fori_loop(2, NB // 2, pack_other, 0)
+    pack(2)
+    pack(3)
 
 
     wait_bytes(r2in.at[pl.ds(0, NS - 1)], recv.at[R2_S])
@@ -395,6 +424,7 @@
         rcopy(
             ax.at[1, rows], rx2.at[4 + y], send.at[X2_S], recv.at[X2_S], (z_far * 2 + c, x * 4 + yy)
         )
+    pass_on()
     wait_bytes(r2all.at[pl.ds(0, 3)], recv.at[R3_S])
     rel_row = pl.ds(pl.multiple_of(c * 256 + shard * 16, 16), 16)
     rfin[rel_row, :] = (((r2all[0] + r2all[1]) + r2all[2]) + r2all[3]).astype(BF16)
@@ -474,6 +504,7 @@
     wait_bytes(o_far.at[1], send.at[O2_S])
     wait_bytes(ot_own, send.at[O3_S])
     wait_bytes(arrived.at[pl.ds(0, 63)], send.at[ENT_S])
+    wait_bytes(passing, send.at[FW_S])
     wait_bytes(far_main, send.at[PX_S])
     wait_bytes(far_last, send.at[PY_S])
     wait_bytes(rp_in, send.at[RC_S])
@@ -584,6 +615,7 @@
     ((D, E_DEV), BF16),
     ((NZ * NS, 112, 128), BF16),
     ((NZ * NS, 112, 128), BF16),
+    ((len(FORWARDED), 112, 128), BF16),
     ((NZ * NS, 48, 128), BF16),
     ((NZ * NS, SLOT, 128), BF16),
     ((NB, 256, 128), F32),
@@ -630,8 +662,8 @@
         out_specs=(anywhere,) * 8,
         scratch_shapes=[pltpu.VMEM(shape, dtype) for shape, dtype in SCRATCH]
         + [
-            pltpu.SemaphoreType.DMA((31,)),
-            pltpu.SemaphoreType.DMA((31,)),
+            pltpu.SemaphoreType.DMA((32,)),
+            pltpu.SemaphoreType.DMA((32,)),
             pltpu.SemaphoreType.REGULAR((4,)),
             pltpu.SemaphoreType.DMA((8,)),
             pltpu.SemaphoreType.DMA((NZ,)),

time: 102 us -> 108 us (1.059)
  the two profiles are of different devices: /device:TPU:32 before, /device:TPU:0 now
where the time goes in v4:
time: 108 us; the launch traced here: 106 us
  Pallas kernels  106 us (98%)
    pallas_call x1, Pallas kernels, per_device(): pl.pallas_call(kernel, out_shape=(jax.ShapeDtypeStruct((NZ * NS, 48, 128)...  100 us
    pallas_call x1, Pallas kernels, per_device(): pl.pallas_call(finish, out_shape=(jax.ShapeDtypeStruct((D, ENT_DEV), F32)...  5.44 us

profile of v4, /device:TPU:0, one launch (start us, length us, event | category | flops | bytes accessed | tf_op | source)
XLA Modules:
  0.0 106.3 jit_solution(232913183858048571)
XLA Ops:
  0.6 100.1 %complex_backward.1 = (bf16[64,48,128]{2,1,0:T(8,128)(2,1)}, bf16[64,16,128]{2,1,0:T(8,128)(2,1)}, bf16[64,48,128]{2,1,0:T(8,128)(2,1)}, bf16[64,16,128]{2,1,0:T...) custom-call(bf16[400,512]{1,0:T(8,128)(2,1)} %bitcast.12, ...), custom_call_target="tpu_custom_call" | custom-call | flops 10066329600 | bytes 8388608 | tf_op jit(solution)/shard_map/complex_backward/pallas_call | solution.py:649
  100.7 5.4 %make_outputs.1 = (f32[400,1024]{1,0:T(8,128)}, f32[64,400]{1,0:T(8,128)}, f32[400,512]{1,0:T(8,128)}) custom-call(bf16[64,48,128]{2,1,0:T(8,128)(2,1)} %get-tuple-element.14.main_in, bf16[64,16,128]{2,1,0:T(8,128)(2,1)} %get-tuple-element.15.last_in, bf16[64,48,128]{2,1,0:T(8,128)(2,1)} %get-tuple-element.16.far_main_in, ...), custom_call_target="tpu_custom_call" | custom-call | flops 2147483648 | bytes 6291456 | tf_op jit(solution)/shard_map/make_outputs/pallas_call | solution.py:688

commit v5 on v3

--- a/solution.py
+++ b/solution.py
@@ -366,8 +366,6 @@
         rcopy(rows, r2in.at[shard], send.at[R2_S], recv.at[R2_S], (bucket, ss))
     r2in[shard] = r1b[pl.ds(pl.multiple_of(shard * 16, 16), 16), :]
     neg_block(0)
-    lax.fori_loop(2, NB // 2, pack_other, 0)
-
 
     wait_bytes(r2in.at[pl.ds(0, NS - 1)], recv.at[R2_S])
     r2 = r2in[0].astype(F32)
@@ -377,6 +375,9 @@
     for k in (1, 3, 2):
         zz = lax.rem(z + k, NZ)
         rcopy(r2all.at[z], r2all.at[z], send.at[R3_S], recv.at[R3_S], (zz * 2 + c, shard))
+
+    lax.fori_loop(2, NZ, pack_other, 0)
+
 
     my_rows = pl.ds(pl.multiple_of(shard * NEG_OWN, NEG_OWN), NEG_OWN)
     wait_bytes(rx1.at[pl.ds(0, 3)], recv.at[X1_S])
@@ -395,13 +396,6 @@
         rcopy(
             ax.at[1, rows], rx2.at[4 + y], send.at[X2_S], recv.at[X2_S], (z_far * 2 + c, x * 4 + yy)
         )
-    wait_bytes(r2all.at[pl.ds(0, 3)], recv.at[R3_S])
-    rel_row = pl.ds(pl.multiple_of(c * 256 + shard * 16, 16), 16)
-    rfin[rel_row, :] = (((r2all[0] + r2all[1]) + r2all[2]) + r2all[3]).astype(BF16)
-    for j in range(1, NS):
-        ss = lax.rem(shard + j, NS)
-        rcopy(rfin.at[rel_row], rfin.at[rel_row], send.at[R4_S], recv.at[R4_S], (bucket, ss))
-
     wait_bytes(ry1.at[pl.ds(0, 3)], recv.at[Y1_S])
     for b in range(2):
         total = gy[b, y].astype(F32)
@@ -432,6 +426,13 @@
         rows = az.at[pl.ds(pl.multiple_of(ss * NEG_OWN, NEG_OWN), NEG_OWN)]
         rcopy(rows, rz2.at[shard], send.at[Z2_S], recv.at[Z2_S], (bucket, ss))
     rz2[shard] = az[my_rows, :]
+
+    wait_bytes(r2all.at[pl.ds(0, 3)], recv.at[R3_S])
+    rel_row = pl.ds(pl.multiple_of(c * 256 + shard * 16, 16), 16)
+    rfin[rel_row, :] = (((r2all[0] + r2all[1]) + r2all[2]) + r2all[3]).astype(BF16)
+    for j in range(1, NS):
+        ss = lax.rem(shard + j, NS)
+        rcopy(rfin.at[rel_row], rfin.at[rel_row], send.at[R4_S], recv.at[R4_S], (bucket, ss))
 
     def give(src, dst, sem):
         pltpu.make_async_copy(src, dst, sem).start()

time: 102 us -> 98 us (0.961)
  the two profiles are of different devices: /device:TPU:32 before, /device:TPU:0 now
where the time goes in v5:
time: 98 us; the launch traced here: 96.9 us
  Pallas kernels  96.1 us (98%)
    pallas_call x1, Pallas kernels, per_device(): pl.pallas_call(kernel, out_shape=(jax.ShapeDtypeStruct((NZ * NS, 48, 128)...  90.7 us
    pallas_call x1, Pallas kernels, per_device(): pl.pallas_call(finish, out_shape=(jax.ShapeDtypeStruct((D, ENT_DEV), F32)...  5.44 us

profile of v5, /device:TPU:0, one launch (start us, length us, event | category | flops | bytes accessed | tf_op | source)
XLA Modules:
  0.0 96.9 jit_solution(14650954003492738684)
XLA Ops:
  0.6 90.7 %complex_backward.1 = (bf16[64,48,128]{2,1,0:T(8,128)(2,1)}, bf16[64,16,128]{2,1,0:T(8,128)(2,1)}, bf16[64,48,128]{2,1,0:T(8,128)(2,1)}, bf16[64,16,128]{2,1,0:T...) custom-call(bf16[400,512]{1,0:T(8,128)(2,1)} %bitcast.12, ...), custom_call_target="tpu_custom_call" | custom-call | flops 10066329600 | bytes 8388608 | tf_op jit(solution)/shard_map/complex_backward/pallas_call | solution.py:618
  91.3 5.4 %make_outputs.1 = (f32[400,1024]{1,0:T(8,128)}, f32[64,400]{1,0:T(8,128)}, f32[400,512]{1,0:T(8,128)}) custom-call(bf16[64,48,128]{2,1,0:T(8,128)(2,1)} %get-tuple-element.14.main_in, bf16[64,16,128]{2,1,0:T(8,128)(2,1)} %get-tuple-element.15.last_in, bf16[64,48,128]{2,1,0:T(8,128)(2,1)} %get-tuple-element.16.far_main_in, ...), custom_call_target="tpu_custom_call" | custom-call | flops 2147483648 | bytes 6291456 | tf_op jit(solution)/shard_map/make_outputs/pallas_call | solution.py:657

commit v6 on v5

--- a/solution.py
+++ b/solution.py
@@ -27,7 +27,7 @@
 
 (Q1_S, SQ1_S, Q2_S, SQ2_S, Q3_S, SQ3_S, ST1_S, O1_S, SC1_S, O2_S, ST2_S, O3_S, SC2_S,
  RC_S, R2_S, R3_S, R4_S, R5_S, ENT_S, Z1_S, X1_S, Y1_S, Z2_S, X2_S, Y2_S, GZ_S, GX_S, GY_S, O4_S,
- PX_S, PY_S) = range(31)
+ PX_S, PY_S, ZX_S) = range(32)
 
 
 def nt(a, b):
@@ -56,7 +56,7 @@
     nbt, wide, nb, prob, qt, sq, hts, tts, rts, mb, st, st_in, sc, sc_in,
     ot, ot_pair, ot_own, o_sum, o_far, lt, qs, ends, rt_hi, rt_lo,
     packed, arrived, far_main, far_last, slot_col, dest_col,
-    gz, gx, gy, rz1, rx1, ry1, az, ax, ay, rz2, rx2, ry2,
+    gz, gx, gy, rz1, rx1, ry1, azx, rzx, az, ax, ay, rz2, rx2, ry2,
     rp, rp_in, r1b, r2in, r2all, rfin,
     send, recv, known, out_sem, ent_recv,
 ):
@@ -154,8 +154,9 @@
     def block(b, two):
 
         chunks = (2 * two, 2 * two + 1)
-        scores = [nn(nb[...], qt[g]) for g in chunks]
-        for g, s in zip(chunks, scores):
+        scores = nn(nb[...], jnp.concatenate([qt[g] for g in chunks], axis=1))
+        for u, g in enumerate(chunks):
+            s = scores[:, u * EC : (u + 1) * EC]
             m = jnp.max(s, axis=0, keepdims=True)
             pb = jnp.exp(s - m).astype(BF16)
             prob[b, :, pl.ds(pl.multiple_of(g * EC, EC), EC)] = pb
@@ -367,6 +368,14 @@
     r2in[shard] = r1b[pl.ds(pl.multiple_of(shard * 16, 16), 16), :]
     neg_block(0)
 
+    wait_bytes(rz1, recv.at[Z1_S])
+    for r in range(4):
+        rr = slice(r * 256, (r + 1) * 256)
+        azx[r] = (gz[0, :, rr].astype(F32) + rz1[:, rr].astype(F32)).astype(BF16)
+    for i in (1, 3, 2):
+        xx = lax.rem(x + i, 4)
+        rcopy(azx.at[xx], rzx.at[x], send.at[ZX_S], recv.at[ZX_S], (bucket, xx * 4 + y))
+
     wait_bytes(r2in.at[pl.ds(0, NS - 1)], recv.at[R2_S])
     r2 = r2in[0].astype(F32)
     for i in range(1, NS):
@@ -379,7 +388,6 @@
     lax.fori_loop(2, NZ, pack_other, 0)
 
 
-    my_rows = pl.ds(pl.multiple_of(shard * NEG_OWN, NEG_OWN), NEG_OWN)
     wait_bytes(rx1.at[pl.ds(0, 3)], recv.at[X1_S])
     for b in range(2):
         total = gx[b, x].astype(F32)
@@ -411,21 +419,19 @@
         rcopy(
             ay.at[1, xx], ry2.at[4 + x], send.at[Y2_S], recv.at[Y2_S], (z_far * 2 + c, xx * 4 + y)
         )
-    wait_bytes(rz1, recv.at[Z1_S])
-
-    def sum_z(r, carry):
-        rr = pl.ds(pl.multiple_of(r * 256, 256), 256)
-        total = gz[0, :, rr].astype(F32) + rz1[:, rr].astype(F32)
-        wide_sum = jnp.concatenate([total, jnp.zeros((256 - (D - 256), 256), F32)], axis=0)
-        az[rr, :] = wide_sum.T.astype(BF16)
-        return carry
-
-    lax.fori_loop(0, 4, sum_z, 0)
-    for j in range(1, NS):
-        ss = lax.rem(shard + j, NS)
-        rows = az.at[pl.ds(pl.multiple_of(ss * NEG_OWN, NEG_OWN), NEG_OWN)]
-        rcopy(rows, rz2.at[shard], send.at[Z2_S], recv.at[Z2_S], (bucket, ss))
-    rz2[shard] = az[my_rows, :]
+    wait_bytes(rzx.at[pl.ds(0, 3)], recv.at[ZX_S])
+    total = azx[x].astype(F32)
+    for i in range(1, 4):
+        total = total + rzx[lax.rem(x + i, 4)].astype(F32)
+    wide_sum = jnp.concatenate([total, jnp.zeros((256 - (D - 256), 256), F32)], axis=0)
+    az[...] = wide_sum.T.astype(BF16)
+    for i in range(4):
+        yy = lax.rem(y + i, 4)
+        rows = pl.ds(pl.multiple_of(yy * NEG_OWN, NEG_OWN), NEG_OWN)
+        if i:
+            rcopy(az.at[rows], rz2.at[y], send.at[Z2_S], recv.at[Z2_S], (bucket, x * 4 + yy))
+        else:
+            rz2[y] = az[rows, :]
 
     wait_bytes(r2all.at[pl.ds(0, 3)], recv.at[R3_S])
     rel_row = pl.ds(pl.multiple_of(c * 256 + shard * 16, 16), 16)
@@ -452,7 +458,7 @@
     give(rx2, rx2_out, out_sem.at[1])
     wait_bytes(ry2.at[pl.ds(0, 7)], recv.at[Y2_S])
     give(ry2, ry2_out, out_sem.at[2])
-    wait_bytes(rz2.at[pl.ds(0, NS - 1)], recv.at[Z2_S])
+    wait_bytes(rz2.at[pl.ds(0, 3)], recv.at[Z2_S])
     give(rz2, rz2_out, out_sem.at[3])
     wait_bytes(half_rel, recv.at[R5_S])
     give(rfin, rel_sum_out, out_sem.at[4])
@@ -487,7 +493,8 @@
     wait_bytes(ry1.at[pl.ds(0, 3)], send.at[Y1_S])
     wait_bytes(rx2.at[pl.ds(0, 7)], send.at[X2_S])
     wait_bytes(ry2.at[pl.ds(0, 7)], send.at[Y2_S])
-    wait_bytes(rz2.at[pl.ds(0, NS - 1)], send.at[Z2_S])
+    wait_bytes(rz2.at[pl.ds(0, 3)], send.at[Z2_S])
+    wait_bytes(rzx.at[pl.ds(0, 3)], send.at[ZX_S])
     for number in (0, 6):
         wait_bytes(far_main, out_sem.at[number])
     for number in (5, 7):
@@ -595,10 +602,12 @@
     ((D - 256, NEG_DEV), BF16),
     ((4, 2, 256, 128), BF16),
     ((4, 2, 4, NEG_OWN, 128), BF16),
-    ((NEG_DEV, 256), BF16),
+    ((4, D - 256, 256), BF16),
+    ((4, D - 256, 256), BF16),
+    ((256, 256), BF16),
     ((2, 256, 128), BF16),
     ((2, 4, NEG_OWN, 128), BF16),
-    ((NS, NEG_OWN, 256), BF16),
+    ((4, NEG_OWN, 256), BF16),
     ((8, NEG_OWN, 128), BF16),
     ((8, NEG_OWN, 128), BF16),
     ((REL, D), F32),
@@ -624,15 +633,15 @@
             jax.ShapeDtypeStruct((NZ * NS, SLOT, 128), BF16),
             jax.ShapeDtypeStruct((8, NEG_OWN, 128), BF16),
             jax.ShapeDtypeStruct((8, NEG_OWN, 128), BF16),
-            jax.ShapeDtypeStruct((NS, NEG_OWN, 256), BF16),
+            jax.ShapeDtypeStruct((4, NEG_OWN, 256), BF16),
             jax.ShapeDtypeStruct((REL, D), BF16),
         ),
         in_specs=[vmem] * 8,
         out_specs=(anywhere,) * 8,
         scratch_shapes=[pltpu.VMEM(shape, dtype) for shape, dtype in SCRATCH]
         + [
-            pltpu.SemaphoreType.DMA((31,)),
-            pltpu.SemaphoreType.DMA((31,)),
+            pltpu.SemaphoreType.DMA((32,)),
+            pltpu.SemaphoreType.DMA((32,)),
             pltpu.SemaphoreType.REGULAR((4,)),
             pltpu.SemaphoreType.DMA((8,)),
             pltpu.SemaphoreType.DMA((NZ,)),
@@ -670,7 +679,7 @@
             pltpu.VMEM((NZ * NS, SLOT, 128), BF16),
             pltpu.VMEM((8, NEG_OWN, 128), BF16),
             pltpu.VMEM((8, NEG_OWN, 128), BF16),
-            pltpu.VMEM((NS, NEG_OWN, 256), BF16),
+            pltpu.VMEM((4, NEG_OWN, 256), BF16),
             pltpu.VMEM((REL, D), BF16),
             pltpu.VMEM((2, D, 512), F32),
             pltpu.VMEM((NEG_OWN, D), F32),

time: 98 us -> 97.7 us (level)
  the two profiles are of different devices: /device:TPU:0 before, /device:TPU:33 now
where the time goes in v6:
time: 97.7 us; the launch traced here: 97.5 us
  Pallas kernels  96.7 us (99%)
    pallas_call x1, Pallas kernels, per_device(): pl.pallas_call(kernel, out_shape=(jax.ShapeDtypeStruct((NZ * NS, 48, 128)...  91.3 us
    pallas_call x1, Pallas kernels, per_device(): pl.pallas_call(finish, out_shape=(jax.ShapeDtypeStruct((D, ENT_DEV), F32)...  5.44 us

profile of v6, /device:TPU:33, one launch (start us, length us, event | category | flops | bytes accessed | tf_op | source)
XLA Modules:
  0.0 97.5 jit_solution(5910375939621591232)
XLA Ops:
  0.6 91.3 %complex_backward.1 = (bf16[64,48,128]{2,1,0:T(8,128)(2,1)}, bf16[64,16,128]{2,1,0:T(8,128)(2,1)}, bf16[64,48,128]{2,1,0:T(8,128)(2,1)}, bf16[64,16,128]{2,1,0:T...) custom-call(bf16[400,512]{1,0:T(8,128)(2,1)} %bitcast.12, ...), custom_call_target="tpu_custom_call" | custom-call | flops 10066329600 | bytes 8388608 | tf_op jit(solution)/shard_map/complex_backward/pallas_call | solution.py:627
  91.9 5.4 %make_outputs.1 = (f32[400,1024]{1,0:T(8,128)}, f32[64,400]{1,0:T(8,128)}, f32[400,512]{1,0:T(8,128)}) custom-call(bf16[64,48,128]{2,1,0:T(8,128)(2,1)} %get-tuple-element.14.main_in, bf16[64,16,128]{2,1,0:T(8,128)(2,1)} %get-tuple-element.15.last_in, bf16[64,48,128]{2,1,0:T(8,128)(2,1)} %get-tuple-element.16.far_main_in, ...), custom_call_target="tpu_custom_call" | custom-call | flops 2147483648 | bytes 6291456 | tf_op jit(solution)/shard_map/make_outputs/pallas_call | solution.py:666

commit v7 on v6

--- a/solution.py
+++ b/solution.py
@@ -51,14 +51,14 @@
 
 
 def kernel(
-    head, tail, ids, rel, wts, neg, slots, drows,
+    head_in, tail_in, ids, rel_in, wts, neg_in, slots, drows,
     main_out, last_out, far_main_out, far_last_out, rx2_out, ry2_out, rz2_out, rel_sum_out,
-    nbt, wide, nb, prob, qt, sq, hts, tts, rts, mb, st, st_in, sc, sc_in,
+    head, tail, rel, neg, nbt, wide, nb, prob, qt, sq, hts, tts, rts, mb, st, st_in, sc, sc_in,
     ot, ot_pair, ot_own, o_sum, o_far, lt, qs, ends, rt_hi, rt_lo,
     packed, arrived, far_main, far_last, slot_col, dest_col,
     gz, gx, gy, rz1, rx1, ry1, azx, rzx, az, ax, ay, rz2, rx2, ry2,
     rp, rp_in, r1b, r2in, r2all, rfin,
-    send, recv, known, out_sem, ent_recv,
+    send, recv, known, out_sem, ent_recv, in_sem,
 ):
     bucket, shard = lax.axis_index("bucket"), lax.axis_index("shard")
     z, c = bucket // 2, bucket % 2
@@ -85,15 +85,20 @@
         for device in devices:
             pl.semaphore_signal(sem, inc=1, device_id=device, device_id_type=MESH)
 
+    loads = [
+        pltpu.make_async_copy(src, dst, in_sem.at[i])
+        for i, (src, dst) in enumerate(((rel_in, rel), (head_in, head), (tail_in, tail), (neg_in, neg)))
+    ]
+    for load in loads:
+        load.start()
     tell(barrier, friends)
 
     for g in range(8):
         qt[g, D:DP, :] = jnp.zeros((DP - D, EC), BF16)
     wide[D:, :] = jnp.ones((16, NEG_DEV), BF16)
 
-    for i in range(8):
-        nbt[i] = neg[:, i * 128 : (i + 1) * 128]
-
+    for load in loads[0:3]:
+        load.wait()
     rel_1 = rel[...].astype(BF16)
     rest = rel[...] - rel_1.astype(F32)
     rel_2 = rest.astype(BF16)
@@ -114,6 +119,10 @@
         hts[j] = h_t
         tts[j] = t_t
         rts[j] = r_t
+
+    loads[3].wait()
+    for i in range(8):
+        nbt[i] = neg[:, i * 128 : (i + 1) * 128]
 
     pl.semaphore_wait(barrier, len(friends))
     tell(known.at[0], y_peers)
@@ -177,6 +186,28 @@
                 st[g, 0:1, :] = m_new
                 st[g, 1:2, :] = st[g, 1:2, :] * f_old + l * f_new
                 ot[g] = ot[g] * f_old + o * f_new
+
+    def score_far(two):
+        chunks = (2 * two, 2 * two + 1)
+        scores = nn(nb[...], jnp.concatenate([qt[g] for g in chunks], axis=1))
+        for u, g in enumerate(chunks):
+            s = scores[:, u * EC : (u + 1) * EC]
+            m = jnp.max(s, axis=0, keepdims=True)
+            p = jnp.exp(s - m)
+            prob[1, :, pl.ds(pl.multiple_of(g * EC, EC), EC)] = p.astype(BF16)
+            l = jnp.sum(p, axis=0, keepdims=True)
+            mb[1, g, 0:1, :] = m
+            m_old = mb[0, g, 0:1, :]
+            m_new = jnp.maximum(m_old, m)
+            st[g, 0:1, :] = m_new
+            st[g, 1:2, :] = st[g, 1:2, :] * jnp.exp(m_old - m_new) + l * jnp.exp(m - m_new)
+
+    def sum_far(two):
+        for g in (2 * two, 2 * two + 1):
+            o = nn(wide[0:D, :], prob[1, :, pl.ds(pl.multiple_of(g * EC, EC), EC)])
+            m_old, m = mb[0, g, 0:1, :], mb[1, g, 0:1, :]
+            m_new = jnp.maximum(m_old, m)
+            ot[g] = ot[g] * jnp.exp(m_old - m_new) + o * jnp.exp(m - m_new)
 
     flip(0)
     block(0, c)
@@ -222,7 +253,10 @@
         sc[g, 2:8, :] = jnp.zeros((6, EC), F32)
         return f_a, f_b
 
-    block(1, oc)
+    score_far(oc)
+    score_far(c)
+    rcopy(st.at[own_half], st_in.at[own_half], send.at[ST2_S], recv.at[ST2_S], partner)
+    sum_far(oc)
     pl.semaphore_wait(known.at[3], 1)
     rcopy(ot.at[pl.ds(2 * oc, 2)], ot_own, send.at[O3_S], recv.at[O3_S], partner)
     wait_bytes(st_in.at[pair_half], recv.at[ST1_S])
@@ -234,13 +268,12 @@
         o_sum[j] = (ot[4 + 2 * c + j] * f_a + ot_pair[j] * f_b).astype(BF16)
     rcopy(o_sum.at[0], o_far.at[0], send.at[O4_S], recv.at[O4_S], pair)
     rcopy(sc.at[pair_half], sc_in.at[own_half], send.at[SC1_S], recv.at[SC1_S], pair)
-    block(1, c)
-    rcopy(st.at[own_half], st_in.at[own_half], send.at[ST2_S], recv.at[ST2_S], partner)
     wait_bytes(st_in.at[own_half], recv.at[ST2_S])
     for g in range(4):
         merge(g)
     rcopy(sc.at[own_half], sc_in.at[pair_half], send.at[SC2_S], recv.at[SC2_S], pair)
     rcopy(o_sum.at[1], o_far.at[1], send.at[O2_S], recv.at[O2_S], pair)
+    sum_far(c)
     wait_bytes(sc_in.at[own_half], recv.at[SC1_S])
     wait_bytes(sc_in.at[pair_half], recv.at[SC2_S])
     for g in range(8):
@@ -387,6 +420,13 @@
 
     lax.fori_loop(2, NZ, pack_other, 0)
 
+
+    wait_bytes(r2all.at[pl.ds(0, 3)], recv.at[R3_S])
+    rel_row = pl.ds(pl.multiple_of(c * 256 + shard * 16, 16), 16)
+    rfin[rel_row, :] = (((r2all[0] + r2all[1]) + r2all[2]) + r2all[3]).astype(BF16)
+    for j in range(1, NS):
+        ss = lax.rem(shard + j, NS)
+        rcopy(rfin.at[rel_row], rfin.at[rel_row], send.at[R4_S], recv.at[R4_S], (bucket, ss))
 
     wait_bytes(rx1.at[pl.ds(0, 3)], recv.at[X1_S])
     for b in range(2):
@@ -433,13 +473,6 @@
         else:
             rz2[y] = az[rows, :]
 
-    wait_bytes(r2all.at[pl.ds(0, 3)], recv.at[R3_S])
-    rel_row = pl.ds(pl.multiple_of(c * 256 + shard * 16, 16), 16)
-    rfin[rel_row, :] = (((r2all[0] + r2all[1]) + r2all[2]) + r2all[3]).astype(BF16)
-    for j in range(1, NS):
-        ss = lax.rem(shard + j, NS)
-        rcopy(rfin.at[rel_row], rfin.at[rel_row], send.at[R4_S], recv.at[R4_S], (bucket, ss))
-
     def give(src, dst, sem):
         pltpu.make_async_copy(src, dst, sem).start()
 
@@ -566,6 +599,10 @@
 
 
 SCRATCH = [
+    ((D, E_DEV), BF16),
+    ((D, E_DEV), BF16),
+    ((D, REL), F32),
+    ((D, NEG_DEV), BF16),
     ((16, D, 128), BF16),
     ((D + 16, NEG_DEV), BF16),
     ((NEG_DEV, DP), BF16),
@@ -636,7 +673,7 @@
             jax.ShapeDtypeStruct((4, NEG_OWN, 256), BF16),
             jax.ShapeDtypeStruct((REL, D), BF16),
         ),
-        in_specs=[vmem] * 8,
+        in_specs=[anywhere, anywhere, vmem, anywhere, vmem, anywhere, vmem, vmem],
         out_specs=(anywhere,) * 8,
         scratch_shapes=[pltpu.VMEM(shape, dtype) for shape, dtype in SCRATCH]
         + [
@@ -645,6 +682,7 @@
             pltpu.SemaphoreType.REGULAR((4,)),
             pltpu.SemaphoreType.DMA((8,)),
             pltpu.SemaphoreType.DMA((NZ,)),
+            pltpu.SemaphoreType.DMA((4,)),
         ],
         compiler_params=pltpu.CompilerParams(
             collective_id=0, has_side_effects=True, vmem_limit_bytes=60 * 1024 * 1024

time: 97.7 us -> 100 us (1.024)
  Pallas kernels: 96.7 us -> 99.2 us
    pallas_call x1, Pallas kernels: 91.3 us -> 93.7 us  [per_device(): pl.pallas_call(kernel, out_shape=(jax.ShapeDtypeStruct((NZ * NS, 48, 128)...]
where the time goes in v7:
time: 100 us
  Pallas kernels  99.2 us (99%)
    pallas_call x1, Pallas kernels, per_device(): pl.pallas_call(kernel, out_shape=(jax.ShapeDtypeStruct((NZ * NS, 48, 128)...  93.7 us
    pallas_call x1, Pallas kernels, per_device(): pl.pallas_call(finish, out_shape=(jax.ShapeDtypeStruct((D, ENT_DEV), F32)...  5.44 us

profile of v7, /device:TPU:33, one launch (start us, length us, event | category | flops | bytes accessed | tf_op | source)
XLA Modules:
  0.0 100.0 jit_solution(7728693821427627792)
XLA Ops:
  0.6 93.7 %complex_backward.1 = (bf16[64,48,128]{2,1,0:T(8,128)(2,1)}, bf16[64,16,128]{2,1,0:T(8,128)(2,1)}, bf16[64,48,128]{2,1,0:T(8,128)(2,1)}, bf16[64,16,128]{2,1,0:T...) custom-call(bf16[400,512]{1,0:T(8,128)(2,1)} %bitcast.12, ...), custom_call_target="tpu_custom_call" | custom-call | flops 10066329600 | bytes 8388608 | tf_op jit(solution)/shard_map/complex_backward/pallas_call | solution.py:664
  94.4 5.4 %make_outputs.1 = (f32[400,1024]{1,0:T(8,128)}, f32[64,400]{1,0:T(8,128)}, f32[400,512]{1,0:T(8,128)}) custom-call(bf16[64,48,128]{2,1,0:T(8,128)(2,1)} %get-tuple-element.14.main_in, bf16[64,16,128]{2,1,0:T(8,128)(2,1)} %get-tuple-element.15.last_in, bf16[64,48,128]{2,1,0:T(8,128)(2,1)} %get-tuple-element.16.far_main_in, ...), custom_call_target="tpu_custom_call" | custom-call | flops 2147483648 | bytes 6291456 | tf_op jit(solution)/shard_map/make_outputs/pallas_call | solution.py:704

commit v8 on v7

--- a/solution.py
+++ b/solution.py
@@ -420,13 +420,6 @@
 
     lax.fori_loop(2, NZ, pack_other, 0)
 
-
-    wait_bytes(r2all.at[pl.ds(0, 3)], recv.at[R3_S])
-    rel_row = pl.ds(pl.multiple_of(c * 256 + shard * 16, 16), 16)
-    rfin[rel_row, :] = (((r2all[0] + r2all[1]) + r2all[2]) + r2all[3]).astype(BF16)
-    for j in range(1, NS):
-        ss = lax.rem(shard + j, NS)
-        rcopy(rfin.at[rel_row], rfin.at[rel_row], send.at[R4_S], recv.at[R4_S], (bucket, ss))
 
     wait_bytes(rx1.at[pl.ds(0, 3)], recv.at[X1_S])
     for b in range(2):
@@ -472,6 +465,13 @@
             rcopy(az.at[rows], rz2.at[y], send.at[Z2_S], recv.at[Z2_S], (bucket, x * 4 + yy))
         else:
             rz2[y] = az[rows, :]
+
+    wait_bytes(r2all.at[pl.ds(0, 3)], recv.at[R3_S])
+    rel_row = pl.ds(pl.multiple_of(c * 256 + shard * 16, 16), 16)
+    rfin[rel_row, :] = (((r2all[0] + r2all[1]) + r2all[2]) + r2all[3]).astype(BF16)
+    for j in range(1, NS):
+        ss = lax.rem(shard + j, NS)
+        rcopy(rfin.at[rel_row], rfin.at[rel_row], send.at[R4_S], recv.at[R4_S], (bucket, ss))
 
     def give(src, dst, sem):
         pltpu.make_async_copy(src, dst, sem).start()

time: 100 us -> 98.9 us (0.989)
  Pallas kernels: 99.2 us -> 97.9 us
    pallas_call x1, Pallas kernels: 93.7 us -> 92.4 us  [per_device(): pl.pallas_call(kernel, out_shape=(jax.ShapeDtypeStruct((NZ * NS, 48, 128)...]
where the time goes in v8:
time: 98.9 us; the launch traced here: 98.7 us
  Pallas kernels  97.9 us (99%)
    pallas_call x1, Pallas kernels, per_device(): pl.pallas_call(kernel, out_shape=(jax.ShapeDtypeStruct((NZ * NS, 48, 128)...  92.4 us
    pallas_call x1, Pallas kernels, per_device(): pl.pallas_call(finish, out_shape=(jax.ShapeDtypeStruct((D, ENT_DEV), F32)...  5.44 us

profile of v8, /device:TPU:33, one launch (start us, length us, event | category | flops | bytes accessed | tf_op | source)
XLA Modules:
  0.0 98.7 jit_solution(14963116736539937846)
XLA Ops:
  0.6 92.4 %complex_backward.1 = (bf16[64,48,128]{2,1,0:T(8,128)(2,1)}, bf16[64,16,128]{2,1,0:T(8,128)(2,1)}, bf16[64,48,128]{2,1,0:T(8,128)(2,1)}, bf16[64,16,128]{2,1,0:T...) custom-call(bf16[400,512]{1,0:T(8,128)(2,1)} %bitcast.12, ...), custom_call_target="tpu_custom_call" | custom-call | flops 10066329600 | bytes 8388608 | tf_op jit(solution)/shard_map/complex_backward/pallas_call | solution.py:664
  93.1 5.4 %make_outputs.1 = (f32[400,1024]{1,0:T(8,128)}, f32[64,400]{1,0:T(8,128)}, f32[400,512]{1,0:T(8,128)}) custom-call(bf16[64,48,128]{2,1,0:T(8,128)(2,1)} %get-tuple-element.14.main_in, bf16[64,16,128]{2,1,0:T(8,128)(2,1)} %get-tuple-element.15.last_in, bf16[64,48,128]{2,1,0:T(8,128)(2,1)} %get-tuple-element.16.far_main_in, ...), custom_call_target="tpu_custom_call" | custom-call | flops 2147483648 | bytes 6291456 | tf_op jit(solution)/shard_map/make_outputs/pallas_call | solution.py:704

commit v9 on v6

--- a/solution.py
+++ b/solution.py
@@ -357,7 +357,6 @@
         return carry
 
     pack(0, True)
-    lax.fori_loop(1, 2, pack_other, 0)
 
     wait_bytes(rp_in, recv.at[RC_S])
     r1b[...] = (rp[pl.ds(pl.multiple_of(c * 256, 256), 256), :] + rp_in[...]).astype(BF16)
@@ -366,6 +365,7 @@
         rows = r1b.at[pl.ds(pl.multiple_of(ss * 16, 16), 16)]
         rcopy(rows, r2in.at[shard], send.at[R2_S], recv.at[R2_S], (bucket, ss))
     r2in[shard] = r1b[pl.ds(pl.multiple_of(shard * 16, 16), 16), :]
+    lax.fori_loop(1, 2, pack_other, 0)
     neg_block(0)
 
     wait_bytes(rz1, recv.at[Z1_S])

time: 97.7 us -> 94.5 us (0.967)
  the two profiles are of different devices: /device:TPU:33 before, /device:TPU:0 now
where the time goes in v9:
time: 94.5 us; the launch traced here: 94 us
  Pallas kernels  93.2 us (99%)
    pallas_call x1, Pallas kernels, per_device(): pl.pallas_call(kernel, out_shape=(jax.ShapeDtypeStruct((NZ * NS, 48, 128)...  87.8 us
    pallas_call x1, Pallas kernels, per_device(): pl.pallas_call(finish, out_shape=(jax.ShapeDtypeStruct((D, ENT_DEV), F32)...  5.44 us

profile of v9, /device:TPU:0, one launch (start us, length us, event | category | flops | bytes accessed | tf_op | source)
XLA Modules:
  0.0 94.0 jit_solution(1209467468458867933)
XLA Ops:
  0.6 87.8 %complex_backward.1 = (bf16[64,48,128]{2,1,0:T(8,128)(2,1)}, bf16[64,16,128]{2,1,0:T(8,128)(2,1)}, bf16[64,48,128]{2,1,0:T(8,128)(2,1)}, bf16[64,16,128]{2,1,0:T...) custom-call(bf16[400,512]{1,0:T(8,128)(2,1)} %bitcast.12, ...), custom_call_target="tpu_custom_call" | custom-call | flops 10066329600 | bytes 8388608 | tf_op jit(solution)/shard_map/complex_backward/pallas_call | solution.py:627
  88.4 5.4 %make_outputs.1 = (f32[400,1024]{1,0:T(8,128)}, f32[64,400]{1,0:T(8,128)}, f32[400,512]{1,0:T(8,128)}) custom-call(bf16[64,48,128]{2,1,0:T(8,128)(2,1)} %get-tuple-element.14.main_in, bf16[64,16,128]{2,1,0:T(8,128)(2,1)} %get-tuple-element.15.last_in, bf16[64,48,128]{2,1,0:T(8,128)(2,1)} %get-tuple-element.16.far_main_in, ...), custom_call_target="tpu_custom_call" | custom-call | flops 2147483648 | bytes 6291456 | tf_op jit(solution)/shard_map/make_outputs/pallas_call | solution.py:666

commit v10 on v9

--- a/solution.py
+++ b/solution.py
@@ -356,8 +356,6 @@
         pack(k, False)
         return carry
 
-    pack(0, True)
-
     wait_bytes(rp_in, recv.at[RC_S])
     r1b[...] = (rp[pl.ds(pl.multiple_of(c * 256, 256), 256), :] + rp_in[...]).astype(BF16)
     for j in range(1, NS):
@@ -365,6 +363,8 @@
         rows = r1b.at[pl.ds(pl.multiple_of(ss * 16, 16), 16)]
         rcopy(rows, r2in.at[shard], send.at[R2_S], recv.at[R2_S], (bucket, ss))
     r2in[shard] = r1b[pl.ds(pl.multiple_of(shard * 16, 16), 16), :]
+
+    pack(0, True)
     lax.fori_loop(1, 2, pack_other, 0)
     neg_block(0)
 

time: 94.5 us -> 95.9 us (1.015)
  no operation moved by 1% of the time
where the time goes in v10:
time: 95.9 us; the launch traced here: 94.7 us
  Pallas kernels  93.9 us (98%)
    pallas_call x1, Pallas kernels, per_device(): pl.pallas_call(kernel, out_shape=(jax.ShapeDtypeStruct((NZ * NS, 48, 128)...  88.4 us
    pallas_call x1, Pallas kernels, per_device(): pl.pallas_call(finish, out_shape=(jax.ShapeDtypeStruct((D, ENT_DEV), F32)...  5.44 us

profile of v10, /device:TPU:0, one launch (start us, length us, event | category | flops | bytes accessed | tf_op | source)
XLA Modules:
  0.0 94.7 jit_solution(15045691092989014374)
XLA Ops:
  0.6 88.4 %complex_backward.1 = (bf16[64,48,128]{2,1,0:T(8,128)(2,1)}, bf16[64,16,128]{2,1,0:T(8,128)(2,1)}, bf16[64,48,128]{2,1,0:T(8,128)(2,1)}, bf16[64,16,128]{2,1,0:T...) custom-call(bf16[400,512]{1,0:T(8,128)(2,1)} %bitcast.12, ...), custom_call_target="tpu_custom_call" | custom-call | flops 10066329600 | bytes 8388608 | tf_op jit(solution)/shard_map/complex_backward/pallas_call | solution.py:627
  89.1 5.4 %make_outputs.1 = (f32[400,1024]{1,0:T(8,128)}, f32[64,400]{1,0:T(8,128)}, f32[400,512]{1,0:T(8,128)}) custom-call(bf16[64,48,128]{2,1,0:T(8,128)(2,1)} %get-tuple-element.14.main_in, bf16[64,16,128]{2,1,0:T(8,128)(2,1)} %get-tuple-element.15.last_in, bf16[64,48,128]{2,1,0:T(8,128)(2,1)} %get-tuple-element.16.far_main_in, ...), custom_call_target="tpu_custom_call" | custom-call | flops 2147483648 | bytes 6291456 | tf_op jit(solution)/shard_map/make_outputs/pallas_call | solution.py:666
